TPU v7x, 32 devices: a whole 2x2x4 slice. The times are simulated.
32 devices in a mesh: fsdp: 16 (over z, y, core), dp: 2 (over x).
Axes of the slice: x: 2, y: 2, z: 4, core: 2. Of those that a mesh axis runs over, the one named last changes fastest.
Arguments:
- patches: bfloat16 [32, 576, 768], P(('fsdp', 'dp')), may hold values from -6 to 6
- masks: int32 [32, 576], P(('fsdp', 'dp')), may hold values from 0 to 1
- groups: int32 [32], P(('fsdp', 'dp')), may hold values from 0 to 1
- w_square: float32 [3, 768, 768], P(None, 'fsdp'), may hold values from -0.5 to 0.5
- w_qkv: float32 [768, 2304], P('fsdp'), may hold values from -0.21875 to 0.21875
- w_up: float32 [768, 3072], P('fsdp'), may hold values from -0.21875 to 0.21875
- w_down: float32 [3072, 768], P(None, 'fsdp'), may hold values from -0.109375 to 0.109375
- small: float32 [215, 768], P(None, 'fsdp'), may hold values from -4 to 4
- muon_square: float32 [3, 768, 768], P(None, 'fsdp'), may hold values from -0.0009765625 to 0.0009765625
- muon_qkv: float32 [768, 2304], P('fsdp'), may hold values from -0.0009765625 to 0.0009765625
- muon_up: float32 [768, 3072], P('fsdp'), may hold values from -0.0009765625 to 0.0009765625
- muon_down: float32 [3072, 768], P(None, 'fsdp'), may hold values from -0.0009765625 to 0.0009765625
- adam_first: float32 [215, 768], P(None, 'fsdp'), may hold values from -0.00061035156 to 0.00061035156
- adam_second: float32 [215, 768], P(None, 'fsdp'), may hold values from 5e-10 to 8e-09
Outputs:
- loss_sum: float32 [], replicated
- mask_count: float32 [], replicated
- grad_norm: float32 [], replicated
- new_square: float32 [3, 768, 768], P(None, 'fsdp')
- new_muon_square: float32 [3, 768, 768], P(None, 'fsdp')
- new_qkv: float32 [768, 2304], P('fsdp')
- new_muon_qkv: float32 [768, 2304], P('fsdp')
- new_up: float32 [768, 3072], P('fsdp')
- new_muon_up: float32 [768, 3072], P('fsdp')
- new_down: float32 [3072, 768], P(None, 'fsdp')
- new_muon_down: float32 [3072, 768], P(None, 'fsdp')
- new_small: float32 [215, 768], P(None, 'fsdp')
- new_first: float32 [215, 768], P(None, 'fsdp')
- new_second: float32 [215, 768], P(None, 'fsdp')
All inputs are finite; a program needn't handle non-finite values.
Results may differ from a plain program's by a relative error of at most 0.01225.
The roundings to bfloat16 on the way count: a program that leaves them out, or rounds other values in their place, can miss the bound.
Values may be sent and summed in bfloat16 or wider, within the bound.
No kernel may reach another device: no remote copies, remote signals or barrier semaphores. Data moves between devices by JAX's collectives and lax.ppermute only.
A program may use at most 192 MiB of HBM per device.

v0:
```python
from functools import partial
import math

import jax
import jax.numpy as jnp
from jax import lax
from jax.sharding import PartitionSpec as P

D = 768
FF = 3072
HEADS = 12
HEAD_DIM = 64
GRID = 24
SHORT_GRID = 14
NS_ITERS = 5
STEP = 10
PATCHES = 576
SHORT_PATCHES = 196


layer_eps = 1e-06
coeff_first, coeff_second, coeff_third = (3.4445, -4.775, 2.0315)
momentum_decay = 0.95
muon_rate = 0.15
muon_decay = 0.01
beta_first = 0.9
beta_second = 0.999
adam_rate = 0.3
adam_eps = 1e-08
clip_limit = 0.5
masked_score = -1000000000.0


def interp_table(grid_side, short_side):
    axis_rows = []
    for target in range(grid_side):
        source = (target + 0.5) * short_side / grid_side - 0.5
        source = min(max(source, 0.0), short_side - 1.0)
        below = int(math.floor(source))
        above = min(below + 1, short_side - 1)
        upper_weight = source - below
        table_row = [0.0] * short_side
        table_row[below] += 1.0 - upper_weight
        table_row[above] += upper_weight
        axis_rows.append(table_row)
    axis_table = jnp.asarray(axis_rows, dtype=jnp.float32)
    lookup = jnp.zeros((1 + grid_side * grid_side, 1 + short_side * short_side), jnp.float32)
    lookup = lookup.at[0, 0].set(1.0)
    return lookup.at[1:, 1:].set(jnp.kron(axis_table, axis_table))


def layer_norm(values, gain, shift):
    centred = values - jnp.mean(values, axis=-1, keepdims=True)
    variance = jnp.mean(centred * centred, axis=-1, keepdims=True)
    return centred * lax.rsqrt(variance + layer_eps) * gain + shift


def rounded(values):
    return lax.optimization_barrier(values.astype(jnp.bfloat16))


def orthogonalize(sent):
    widened = sent.astype(jnp.float32)
    frob_norm = jnp.sqrt(jnp.sum(widened * widened))
    current = rounded(widened / (frob_norm + 1e-07))
    for sweep in range(NS_ITERS):
        gram_low = rounded(jnp.dot(current, current.T, preferred_element_type=jnp.float32))
        poly_low = rounded(
            coeff_second * gram_low.astype(jnp.float32)
            + coeff_third * jnp.dot(gram_low, gram_low, preferred_element_type=jnp.float32)
        )
        current = rounded(
            coeff_first * current.astype(jnp.float32)
            + jnp.dot(poly_low, current, preferred_element_type=jnp.float32)
        )
    return current


def attend_forward(query_rows, key_rows, value_rows, key_valid, scaling):
    scores = (
        jnp.einsum("qhd,khd->hqk", query_rows, key_rows, preferred_element_type=jnp.float32)
        * scaling
    )
    scores = jnp.where(key_valid[None, None, :], scores, masked_score)
    peak = jnp.max(scores, axis=-1, keepdims=True)
    expo = jnp.exp(scores - peak)
    total = jnp.sum(expo, axis=-1, keepdims=True)
    probs = expo / total
    context = jnp.einsum(
        "hqk,khd->qhd", probs.astype(jnp.bfloat16), value_rows, preferred_element_type=jnp.float32
    )
    return (context, peak[..., 0] + jnp.log(total[..., 0]))


def attend_backward(query_rows, key_rows, value_rows, grad_context, logsum, key_valid, scaling):
    scores = (
        jnp.einsum("qhd,khd->hqk", query_rows, key_rows, preferred_element_type=jnp.float32)
        * scaling
    )
    scores = jnp.where(key_valid[None, None, :], scores, masked_score)
    probs = jnp.exp(scores - logsum[..., None])
    grad_probs = jnp.einsum(
        "qhd,khd->hqk", grad_context, value_rows, preferred_element_type=jnp.float32
    )
    grad_values = jnp.einsum(
        "hqk,qhd->khd", probs.astype(jnp.bfloat16), grad_context, preferred_element_type=jnp.float32
    )
    grad_scores = probs * (grad_probs - jnp.sum(probs * grad_probs, axis=-1, keepdims=True))
    scores_low = (grad_scores * scaling).astype(jnp.bfloat16)
    grad_query = jnp.einsum(
        "hqk,khd->qhd", scores_low, key_rows, preferred_element_type=jnp.float32
    )
    grad_keys = jnp.einsum(
        "hqk,qhd->khd", scores_low, query_rows, preferred_element_type=jnp.float32
    )
    return (grad_query, grad_keys, grad_values)


def per_device(
    patches,
    masks,
    groups,
    w_square,
    w_qkv,
    w_up,
    w_down,
    small,
    muon_square,
    muon_qkv,
    muon_up,
    muon_down,
    adam_first,
    adam_second,
):
    bfloat = jnp.bfloat16
    square_low, qkv_low, up_low, down_low, small_low = (
        w_square.astype(bfloat),
        w_qkv.astype(bfloat),
        w_up.astype(bfloat),
        w_down.astype(bfloat),
        small.astype(bfloat),
    )
    square, qkv_weight, up_weight, down_weight, small_full = (
        lax.all_gather(square_low, "fsdp", axis=1, tiled=True),
        lax.all_gather(qkv_low, "fsdp", axis=0, tiled=True),
        lax.all_gather(up_low, "fsdp", axis=0, tiled=True),
        lax.all_gather(down_low, "fsdp", axis=1, tiled=True),
        lax.all_gather(small_low, "fsdp", axis=1, tiled=True),
    )
    params_small = small_full.astype(jnp.float32)
    image_count, patch_count, width = patches.shape
    seq_len = patch_count + 1
    up_rows = FF // D
    pos_rows = params_small.shape[0] - 14 - up_rows
    long_rows = groups > 0
    patch_limit = jnp.where(long_rows, PATCHES, SHORT_PATCHES)
    chosen = (masks > 0) & (jnp.arange(patch_count)[None, :] < patch_limit[:, None])
    key_valid = jnp.arange(seq_len)[None, :] < (patch_limit + 1)[:, None]
    lookup = interp_table(GRID, SHORT_GRID)
    scaling = HEAD_DIM ** (-0.5)
    heads_shape = (image_count, seq_len, HEADS, HEAD_DIM)
    embed_pre = jnp.dot(patches, square[0], preferred_element_type=jnp.float32)
    embedded = jnp.where(chosen[..., None], params_small[1], embed_pre + params_small[0])
    position = params_small[14 + up_rows :]
    long_pos = jnp.dot(lookup, position, precision=lax.Precision.HIGHEST)
    short_pos = jnp.pad(position, ((0, seq_len - pos_rows), (0, 0)))
    leading = jnp.broadcast_to(params_small[2], (image_count, 1, width))
    resid_first = jnp.concatenate([leading, embedded], axis=1) + jnp.where(
        long_rows[:, None, None], long_pos, short_pos
    )
    normed_first = layer_norm(resid_first, params_small[3], params_small[4]).astype(bfloat)
    qkv_bias = jnp.concatenate(
        [params_small[12], jnp.zeros((width,), jnp.float32), params_small[13]]
    )
    mixed = jnp.dot(normed_first, qkv_weight, preferred_element_type=jnp.float32) + qkv_bias
    query_rows = mixed[..., :width].astype(bfloat).reshape(heads_shape)
    key_rows = mixed[..., width : 2 * width].astype(bfloat).reshape(heads_shape)
    value_rows = mixed[..., 2 * width :].astype(bfloat).reshape(heads_shape)
    context, logsum = lax.map(
        lambda item: attend_forward(item[0], item[1], item[2], item[3], scaling),
        (query_rows, key_rows, value_rows, key_valid),
    )
    context_low = context.reshape(image_count, seq_len, width).astype(bfloat)
    resid_second = (
        resid_first
        + jnp.dot(context_low, square[1], preferred_element_type=jnp.float32)
        + params_small[5]
    )
    normed_second = layer_norm(resid_second, params_small[6], params_small[7]).astype(bfloat)
    hidden_pre = jnp.dot(
        normed_second, up_weight, preferred_element_type=jnp.float32
    ) + params_small[14 : 14 + up_rows].reshape(-1)
    activ_low = jax.nn.gelu(hidden_pre, approximate=False).astype(bfloat)
    resid_third = (
        resid_second
        + jnp.dot(activ_low, down_weight, preferred_element_type=jnp.float32)
        + params_small[8]
    )
    normed_final = layer_norm(resid_third, params_small[9], params_small[10]).astype(bfloat)
    predicted = (
        jnp.dot(normed_final[:, 1:], square[2], preferred_element_type=jnp.float32)
        + params_small[11]
    )
    residual_error = predicted - patches.astype(jnp.float32)
    chosen_float = chosen.astype(jnp.float32)
    loss_local = jnp.sum(chosen_float[..., None] * residual_error * residual_error)
    loss_sum, mask_count = lax.psum((loss_local, jnp.sum(chosen_float)), ("fsdp", "dp"))
    square, qkv_weight, up_weight, down_weight = (
        lax.all_gather(square_low, "fsdp", axis=1, tiled=True),
        lax.all_gather(qkv_low, "fsdp", axis=0, tiled=True),
        lax.all_gather(up_low, "fsdp", axis=0, tiled=True),
        lax.all_gather(down_low, "fsdp", axis=1, tiled=True),
    )
    grad_pred = 2.0 / mask_count * chosen_float[..., None] * residual_error
    pred_low = grad_pred.astype(bfloat)
    grad_head = jnp.einsum(
        "ipd,ipn->dn", normed_final[:, 1:], pred_low, preferred_element_type=jnp.float32
    )
    grad_head_bias = jnp.sum(grad_pred, axis=(0, 1))
    grad_normed = jnp.einsum("ipn,dn->ipd", pred_low, square[2], preferred_element_type=jnp.float32)
    grad_normed = jnp.pad(grad_normed, ((0, 0), (1, 0), (0, 0)))
    unused, pull_final = jax.vjp(layer_norm, resid_third, params_small[9], params_small[10])
    grad_resid, gain_final, shift_final = pull_final(grad_normed)
    branch_low = grad_resid.astype(bfloat)
    grad_down = jnp.einsum("isf,isd->fd", activ_low, branch_low, preferred_element_type=jnp.float32)
    grad_down_bias = jnp.sum(grad_resid, axis=(0, 1))
    grad_activ = jnp.einsum(
        "isd,fd->isf", branch_low, down_weight, preferred_element_type=jnp.float32
    )
    unused, pull_gelu = jax.vjp(partial(jax.nn.gelu, approximate=False), hidden_pre)
    grad_hidden = pull_gelu(grad_activ)[0]
    hidden_low = grad_hidden.astype(bfloat)
    grad_up = jnp.einsum(
        "isd,isf->df", normed_second, hidden_low, preferred_element_type=jnp.float32
    )
    grad_up_bias = jnp.sum(grad_hidden, axis=(0, 1))
    grad_normed = jnp.einsum(
        "isf,df->isd", hidden_low, up_weight, preferred_element_type=jnp.float32
    )
    unused, pull_second = jax.vjp(layer_norm, resid_second, params_small[6], params_small[7])
    grad_norm_part, gain_second, shift_second = pull_second(grad_normed)
    grad_resid = grad_resid + grad_norm_part
    branch_low = grad_resid.astype(bfloat)
    grad_out = jnp.einsum(
        "isc,isd->cd", context_low, branch_low, preferred_element_type=jnp.float32
    )
    grad_out_bias = jnp.sum(grad_resid, axis=(0, 1))
    grad_context = (
        jnp.einsum("isd,cd->isc", branch_low, square[1], preferred_element_type=jnp.float32)
        .astype(bfloat)
        .reshape(heads_shape)
    )
    grad_query, grad_keys, grad_values = lax.map(
        lambda item: attend_backward(item[0], item[1], item[2], item[3], item[4], item[5], scaling),
        (query_rows, key_rows, value_rows, grad_context, logsum, key_valid),
    )
    flat_shape = (image_count, seq_len, width)
    grad_query = grad_query.reshape(flat_shape)
    grad_values = grad_values.reshape(flat_shape)
    mixed_low = jnp.concatenate(
        [grad_query, grad_keys.reshape(flat_shape), grad_values], axis=-1
    ).astype(bfloat)
    grad_qkv = jnp.einsum(
        "isd,isn->dn", normed_first, mixed_low, preferred_element_type=jnp.float32
    )
    grad_normed = jnp.einsum(
        "isn,dn->isd", mixed_low, qkv_weight, preferred_element_type=jnp.float32
    )
    unused, pull_first = jax.vjp(layer_norm, resid_first, params_small[3], params_small[4])
    grad_norm_part, gain_first, shift_first = pull_first(grad_normed)
    grad_resid = grad_resid + grad_norm_part
    grad_leading = jnp.sum(grad_resid[:, 0], axis=0)
    long_mask = long_rows[:, None, None]
    grad_long = jnp.sum(jnp.where(long_mask, grad_resid, 0.0), axis=0)
    grad_short = jnp.sum(jnp.where(long_mask, 0.0, grad_resid), axis=0)[:pos_rows]
    grad_position = jnp.dot(lookup.T, grad_long, precision=lax.Precision.HIGHEST) + grad_short
    grad_embedded = grad_resid[:, 1:]
    grad_mask_token = jnp.sum(jnp.where(chosen[..., None], grad_embedded, 0.0), axis=(0, 1))
    grad_embed_pre = jnp.where(chosen[..., None], 0.0, grad_embedded)
    grad_patch_bias = jnp.sum(grad_embed_pre, axis=(0, 1))
    grad_patch = jnp.einsum(
        "ipc,ipd->cd", patches, grad_embed_pre.astype(bfloat), preferred_element_type=jnp.float32
    )
    vector_rows = jnp.stack(
        [
            grad_patch_bias,
            grad_mask_token,
            grad_leading,
            gain_first,
            shift_first,
            grad_out_bias,
            gain_second,
            shift_second,
            grad_down_bias,
            gain_final,
            shift_final,
            grad_head_bias,
            grad_query.sum(axis=(0, 1)),
            grad_values.sum(axis=(0, 1)),
        ]
    )
    grad_small = jnp.concatenate(
        [vector_rows, grad_up_bias.reshape(up_rows, width), grad_position], axis=0
    )
    grad_square = jnp.stack([grad_patch, grad_out, grad_head])
    part_square, part_qkv, part_up, part_down, part_small = (
        lax.psum_scatter(grad_square, "fsdp", scatter_dimension=1, tiled=True),
        lax.psum_scatter(grad_qkv, "fsdp", scatter_dimension=0, tiled=True),
        lax.psum_scatter(grad_up, "fsdp", scatter_dimension=0, tiled=True),
        lax.psum_scatter(grad_down, "fsdp", scatter_dimension=1, tiled=True),
        lax.psum_scatter(grad_small, "fsdp", scatter_dimension=1, tiled=True),
    )
    reduced = lax.psum((part_square, part_qkv, part_up, part_down, part_small), "dp")
    local_squares = sum((jnp.sum(item * item) for item in reduced))
    grad_norm = jnp.sqrt(lax.psum(local_squares, "fsdp"))
    factor = jnp.minimum(1.0, clip_limit / (grad_norm + 1e-06))
    clipped = [item * factor for item in reduced]
    momenta = [muon_square, muon_qkv, muon_up, muon_down]
    new_momenta = [momentum_decay * old + fresh for old, fresh in zip(momenta, clipped[:4])]
    blends = [fresh + momentum_decay * moment for fresh, moment in zip(clipped[:4], new_momenta)]
    blend_views = [blends[0][0], blends[0][1], blends[0][2], blends[1], blends[2], blends[3].T]
    view_widths = [view.shape[1] for view in blend_views]
    widest = max(view_widths)
    stacked = jnp.stack(
        [jnp.pad(view, ((0, 0), (0, widest - view.shape[1]))) for view in blend_views]
    ).astype(bfloat)
    dp_size = lax.axis_size("dp")
    dp_index = lax.axis_index("dp")
    fsdp_index = lax.axis_index("fsdp")
    own_rows = stacked.shape[1]
    results = []
    for round_number in range(-(-6 // dp_size)):
        slot = jnp.minimum(round_number * dp_size + dp_index, 5)
        owned = lax.dynamic_index_in_dim(stacked, slot, 0, keepdims=False)
        whole = lax.all_gather(owned, "fsdp", axis=0, tiled=True)
        ortho = orthogonalize(whole)
        own_part = lax.dynamic_slice_in_dim(ortho, fsdp_index * own_rows, own_rows, 0)
        results.append(lax.all_gather(own_part[None], "dp", axis=0, tiled=True))
    updates = jnp.concatenate(results, axis=0)[:6].astype(jnp.float32)
    weight_views = [w_square[0], w_square[1], w_square[2], w_qkv, w_up, w_down.T]
    new_views = []
    for index_number in range(6):
        columns = view_widths[index_number]
        new_views.append(
            weight_views[index_number] * (1.0 - muon_rate * muon_decay)
            - muon_rate * 0.2 * math.sqrt(columns) * updates[index_number][:, :columns]
        )
    small_grad = clipped[4]
    new_first = beta_first * adam_first + (1.0 - beta_first) * small_grad
    new_second = beta_second * adam_second + (1.0 - beta_second) * small_grad * small_grad
    first_hat = new_first / (1.0 - beta_first**STEP)
    second_hat = new_second / (1.0 - beta_second**STEP)
    new_small = small - adam_rate * first_hat / (jnp.sqrt(second_hat) + adam_eps)
    return (
        loss_sum,
        mask_count,
        grad_norm,
        jnp.stack(new_views[:3]),
        new_momenta[0],
        new_views[3],
        new_momenta[1],
        new_views[4],
        new_momenta[2],
        new_views[5].T,
        new_momenta[3],
        new_small,
        new_first,
        new_second,
    )


def solution(mesh):
    placed = (
        P(("fsdp", "dp"), None, None),
        P(("fsdp", "dp"), None),
        P(("fsdp", "dp")),
        P(None, "fsdp", None),
        P("fsdp", None),
        P("fsdp", None),
        P(None, "fsdp"),
        P(None, "fsdp"),
        P(None, "fsdp", None),
        P("fsdp", None),
        P("fsdp", None),
        P(None, "fsdp"),
        P(None, "fsdp"),
        P(None, "fsdp"),
    )
    return jax.shard_map(
        per_device,
        mesh=mesh,
        in_specs=placed,
        out_specs=(
            P(),
            P(),
            P(),
            P(None, "fsdp", None),
            P(None, "fsdp", None),
            P("fsdp", None),
            P("fsdp", None),
            P("fsdp", None),
            P("fsdp", None),
            P(None, "fsdp"),
            P(None, "fsdp"),
            P(None, "fsdp"),
            P(None, "fsdp"),
            P(None, "fsdp"),
        ),
        check_vma=False,
    )
```

profile of v0, /device:TPU:20, one launch (start us, length us, event | category | flops | bytes accessed | tf_op | source)
XLA Modules:
  0.0 1391.0 jit_solution(1106329149208414689)
XLA Ops:
  13.7 16.4 %all_gather.37 = bf16[215,768]{0,1:T(8,128)(2,1)S(1)} all-gather(bf16[215,48]{0,1:T(8,128)(2,1)S(1)} %convert_element_type.354), channel_id=1, replica_groups=mesh['fsdp'=16,'dp'=2] {'fsdp'}, dimensions={1}, use_global_device_ids=true | all-gather | bytes 350880 | tf_op jit(solution)/shard_map/all_gather | solution.py:148
  32.5 45.5 %psum.57 = f32[]{:T(128)} all-reduce(f32[]{:T(128)} %get-tuple-element.185), channel_id=1, replica_groups=mesh['fsdp'=16,'dp'=2] {'fsdp','dp'}, use_global_device_ids=true, to_apply=%region_11.12 | all-reduce | flops 1 | bytes 8 | tf_op jit(solution)/shard_map/psum | solution.py:207
  90.2 18.4 %all-gather.16.cloned.1.call-done = bf16[768,2304]{1,0:T(8,128)(2,1)} async-done(((bf16[48,2304]{1,0:T(8,128)(2,1)}), bf16[768,2304]{1,0:T(8,128)(2,1)}) %all-gather.16.cloned.1.call-update) | async-done | bytes 3538960 | tf_op jit(solution)/shard_map/all_gather | solution.py:145
  125.1 10.0 fusion.2
  135.8 9.4 fusion.45
  148.2 15.1 %all-gather.18.cloned.1.call-done = bf16[768,3072]{1,0:T(8,128)(2,1)} async-done(((bf16[48,3072]{1,0:T(8,128)(2,1)}), bf16[768,3072]{1,0:T(8,128)(2,1)}) %all-gather.18.cloned.1.call-update) | async-done | bytes 4718608 | tf_op jit(solution)/shard_map/all_gather | solution.py:146
  163.3 22.7 %multiply_convert_fusion.1 = (bf16[577,3072]{1,0:T(8,128)(2,1)}, f32[577,3072]{1,0:T(8,128)}, f32[577,3072]{1,0:T(8,128)}) fusion(f32[3072]{0:T(1024)S(1)} %add.396, bf16[768,3072]{1,0:T(8,128)(2,1)} %all-gather.18.cloned.1.call-done, f32[577,768]{1,0:T(8,128)S(1)} %get-tuple-element.237, f32[768]{0:T(1024)S(1)} %get-tuple-element.176, ...), kind=kOutput, calls=%fused_computation.47 | convolution fusion | flops 2841831168 | bytes 24239624 | tf_op jit(solution)/shard_map/dot_general | solution.py:190
  186.1 31.9 %all-gather.20.cloned.1.call-done = bf16[3072,768]{0,1:T(8,128)(2,1)} async-done(((bf16[3072,48]{0,1:T(8,128)(2,1)}), bf16[3072,768]{0,1:T(8,128)(2,1)}) %all-gather.20.cloned.1.call-update) | async-done | bytes 4718608 | tf_op jit(solution)/shard_map/all_gather | solution.py:147
  234.0 10.2 fusion.119
  256.4 10.4 fusion.120
  266.8 11.9 bitcast_convert_fusion
  278.7 31.3 %fusion.46 = bf16[12,64,577]{2,1,0:T(8,128)(2,1)} fusion(bf16[577,12,64]{0,2,1:T(8,128)(2,1)} %bitcast.304, f32[12,577,577]{1,2,0:T(8,128)} %fusion.120, f32[12,577,577]{1,2,0:T(8,128)} %get-tuple-element.235, f32[12,577]{1,0:T(8,128)S(1)} %log_add_fusion, pred[577]{0:T(1024)(128)(4,1)S(1)} %iota_compare_fusion), kind=kOutput, calls=%fused_computation.157 | convolution fusion | flops 555776192 | bytes 33762000 | tf_op jit(solution)/shard_map/while/body/eval_jaxpr/hqk,qhd->khd/dot_general | solution.py:113
  310.0 31.7 %bitcast_convert_fusion.1 = (bf16[577,12,64]{0,2,1:T(8,128)(2,1)}, f32[12,64,577]{2,1,0:T(8,128)}) fusion(bf16[577,12,64]{0,2,1:T(8,128)(2,1)S(1)} %bitcast.302, f32[12,577,577]{1,2,0:T(8,128)} %fusion.120, f32[12,577]{1,0:T(8,128)S(1)} %log_add_fusion, f32[12,577,577]{1,2,0:T(8,128)} %get-tuple-element.235, pred[577]{0:T(1024)(128)(4,1)S(1)} %iota_compare_fusion), kind=kOutput, calls=%fused_computation.91 | convolution fusion | flops 555776192 | bytes 35534544 | tf_op jit(solution)/shard_map/while/body/eval_jaxpr/hqk,khd->qhd/dot_general | solution.py:110
  356.9 11.0 copy.199
  377.5 10.3 convolution_bitcast_fusion
  407.2 145.7 %all-reduce.11.cloned.1.call-done = f32[3,768,768]{2,0,1:T(4,128)} async-done(((f32[3,768,768]{2,0,1:T(4,128)}), f32[3,768,768]{2,0,1:T(4,128)}) %all-reduce.11.cloned.1.call-update) | async-done | bytes 7077904
  554.9 92.2 %reduce-scatter.13.cloned.1.call-done = f32[48,2304]{1,0:T(8,128)} async-done(((f32[768,2304]{1,0:T(8,128)}), f32[48,2304]{1,0:T(8,128)}) %reduce-scatter.13.cloned.1.call-update) | async-done | bytes 442384
  649.5 112.8 %reduce-scatter.17.cloned.1.call-done = f32[48,3072]{1,0:T(8,128)} async-done(((f32[768,3072]{1,0:T(8,128)}), f32[48,3072]{1,0:T(8,128)}) %reduce-scatter.17.cloned.1.call-update) | async-done | bytes 589840
  765.0 113.1 %reduce-scatter.15.cloned.1.call-done = f32[48,3072]{1,0:T(8,128)} async-done(((f32[768,3072]{1,0:T(8,128)}), f32[48,3072]{1,0:T(8,128)}) %reduce-scatter.15.cloned.1.call-update) | async-done | bytes 589840
  886.5 50.7 %reduce-scatter.19.cloned.1.call-done = f32[48,215]{1,0:T(8,128)} async-done(((f32[768,215]{1,0:T(8,128)}), f32[48,215]{1,0:T(8,128)}) %reduce-scatter.19.cloned.1.call-update) | async-done | bytes 41296
  947.0 114.9 %all-reduce.13.cloned.1.call-done = (f32[3,48,768]{2,1,0:T(8,128)}, f32[48,2304]{0,1:T(8,128)}, f32[48,3072]{0,1:T(8,128)}, f32[3072,48]{1,0:T(8,128)}) async-done(((f32[3,48,768]{2,1,0:T(8,128)}, f32[48,2304]{0,1:T(8,128)}, f32[48,3072]{0,1:T(8,128)}, f32[3072,48]{1,0:T(8,128)}), (f32[3,48,768]{2,1,0:T(8,128)}, f32[48,2304]{0,1:T(8,128)}, f32[48,3072]{0,1:T(8,128)}, ...) | async-done | bytes 2064400 | tf_op jit(solution)/shard_map/psum | solution.py:313
  1072.6 21.1 %psum.63 = f32[]{:T(128)} all-reduce(f32[]{:T(128)S(6)} %add.418), channel_id=1, replica_groups=mesh['fsdp'=16,'dp'=2] {'fsdp'}, use_global_device_ids=true, to_apply=%region_48.49 | all-reduce | flops 1 | bytes 8 | tf_op jit(solution)/shard_map/psum | solution.py:315
  1121.4 52.8 %psum.56 = f32[]{:T(128)} all-reduce(f32[]{:T(128)} %get-tuple-element.170), channel_id=1, replica_groups=mesh['fsdp'=16,'dp'=2] {'fsdp','dp'}, use_global_device_ids=true, to_apply=%region_9.10 | all-reduce | flops 1 | bytes 8 | tf_op jit(solution)/shard_map/psum | solution.py:207
  1296.1 9.9 all-gather.5
  (342 shorter events, 366.5 us)
Async XLA Ops:
  7.2 77.9 %all-gather.14.cloned.1.call-start = ((), (), s32[]{:S(2)}) async-start(), calls=%async_computation.4 | async-start | bytes 3760128 | tf_op jit(solution)/shard_map/all_gather | solution.py:144
  9.0 99.5 %all-gather.16.cloned.1.call-start = ((), (), s32[]{:S(2)}) async-start(), calls=%async_computation.5 | async-start | bytes 3760128 | tf_op jit(solution)/shard_map/all_gather | solution.py:145
  10.8 152.5 %all-gather.18.cloned.1.call-start = ((), (), s32[]{:S(2)}) async-start(), calls=%async_computation.6 | async-start | bytes 5013504 | tf_op jit(solution)/shard_map/all_gather | solution.py:146
  12.7 205.3 %all-gather.20.cloned.1.call-start = ((), (), s32[]{:S(2)}) async-start(), calls=%async_computation.7 | async-start | bytes 5013504 | tf_op jit(solution)/shard_map/all_gather | solution.py:147
  13.6 64.6 %copy-start.45 = (f32[24,14]{0,1:T(8,128)S(1)}, f32[24,14]{0,1:T(8,128)}, u32[]{:S(2)}) copy-start(f32[24,14]{0,1:T(8,128)} %constant.278.clone) | copy-start | bytes 4036
  13.6 539.3 %all-reduce.11.cloned.1.call-start = ((), (), s32[]{:S(2)}) async-start(), calls=%async_computation.15 | async-start | bytes 18874368
  78.1 30.4 %copy-start.46 = (f32[768]{0:T(1024)}, f32[768]{0:T(1024)S(1)}, u32[]{:S(2)}) copy-start(f32[768]{0:T(1024)S(1)} %get-tuple-element.182) | copy-start | bytes 9220
  78.1 30.4 %copy-start.52 = (f32[768]{0:T(1024)}, f32[768]{0:T(1024)S(1)}, u32[]{:S(2)}) copy-start(f32[768]{0:T(1024)S(1)} %get-tuple-element.181) | copy-start | bytes 9220
  89.8 23.2 %copy-start = (f32[577,768]{1,0:T(8,128)}, f32[577,768]{1,0:T(8,128)S(1)}, u32[]{:S(2)}) copy-start(f32[577,768]{1,0:T(8,128)S(1)} %get-tuple-element.233) | copy-start | bytes 5317636
  278.7 31.3 %copy-start.18 = (bf16[1,577,768]{1,2,0:T(8,128)(2,1)S(1)}, bf16[1,577,768]{1,2,0:T(8,128)(2,1)}, u32[]{:S(2)}) copy-start(bf16[1,577,768]{1,2,0:T(8,128)(2,1)} %copy-done.17) | copy-start | bytes 2658820
  310.0 31.8 %copy-start.42 = (f32[577]{0:T(1024)S(1)}, f32[577]{0:T(1024)}, u32[]{:S(2)}) copy-start(f32[577]{0:T(1024)} %copy-done.41) | copy-start | bytes 6928
  310.0 31.8 %copy-start.47 = (f32[768]{0:T(1024)S(1)}, f32[768]{0:T(1024)}, u32[]{:S(2)}) copy-start(f32[768]{0:T(1024)} %copy-done.46) | copy-start | bytes 9220
  310.0 31.8 %copy-start.49 = (f32[577]{0:T(1024)S(1)}, f32[577]{0:T(1024)}, u32[]{:S(2)}) copy-start(f32[577]{0:T(1024)} %copy-done.48) | copy-start | bytes 6928
  368.0 279.1 %reduce-scatter.13.cloned.1.call-start = ((), (), s32[]{:S(2)}) async-start(), calls=%async_computation.11 | async-start | bytes 7520256
  377.5 384.8 %reduce-scatter.17.cloned.1.call-start = ((), (), s32[]{:S(2)}) async-start(), calls=%async_computation.13 | async-start | bytes 10027008
  387.8 490.3 %reduce-scatter.15.cloned.1.call-start = ((), (), s32[]{:S(2)}) async-start(), calls=%async_computation.12 | async-start | bytes 10027008
  396.5 540.7 %reduce-scatter.19.cloned.1.call-start = ((), (), s32[]{:S(2)}) async-start(), calls=%async_computation.14 | async-start | bytes 835584
  405.9 656.0 %all-reduce.13.cloned.1.call-start = ((), (), s32[]{:S(2)}) async-start(), calls=%async_computation.16 | async-start | bytes 9535488 | tf_op jit(solution)/shard_map/psum | solution.py:313
  880.9 301.6 %all-gather.26.cloned.1.call-start = ((), (), s32[]{:S(2)}) async-start(), calls=%async_computation.10 | async-start | bytes 5013504 | tf_op jit(solution)/shard_map/all_gather | solution.py:335
  1061.9 32.6 %copy-start.26 = (f32[3,48,768]{2,1,0:T(8,128)S(1)}, f32[3,48,768]{2,1,0:T(8,128)}, u32[]{:S(2)}) copy-start(f32[3,48,768]{2,1,0:T(8,128)} %get-tuple-element.187) | copy-start | bytes 1327108
  1061.9 32.6 %copy-start.35 = (f32[3,48,768]{2,1,0:T(8,128)S(1)}, f32[3,48,768]{2,1,0:T(8,128)}, u32[]{:S(2)}) copy-start(f32[3,48,768]{2,1,0:T(8,128)} %param.27) | copy-start | bytes 1327108
  1116.9 59.7 %copy-start.12 = (f32[48,3072]{0,1:T(8,128)S(1)}, f32[48,3072]{0,1:T(8,128)}, u32[]{:S(2)}) copy-start(f32[48,3072]{0,1:T(8,128)} %get-tuple-element.215) | copy-start | bytes 1769476
  1120.8 118.8 %all-gather.24.cloned.1.call-start = ((), (), s32[]{:S(2)}) async-start(), calls=%async_computation.9 | async-start | bytes 5013504 | tf_op jit(solution)/shard_map/all_gather | solution.py:335
  1121.4 193.6 %all-gather.22.cloned.1.call-start = ((), (), s32[]{:S(2)}) async-start(), calls=%async_computation.8 | async-start | bytes 5013504 | tf_op jit(solution)/shard_map/all_gather | solution.py:335
  (52 other events, 287.9 us)
Sparse Core Ops, SparseCore 0:
  10.9 48.6 all-gather.13
  62.4 46.0 all-gather.15
  111.4 51.9 all-gather.17
  166.1 51.9 all-gather.19
  368.1 184.7 all-reduce.10
  557.3 89.7 reduce-scatter.12
  651.2 111.0 reduce-scatter.16
  767.0 111.1 reduce-scatter.14
  881.7 55.5 reduce-scatter.18
  940.5 121.3 all-reduce.12
  1120.9 61.5 all-gather.25
  1185.4 52.1 all-gather.23
  1240.7 51.9 all-gather.21
where the time goes:
time: 1400 us; the launch traced here: 1390 us
  waiting for transfers between devices  698 us (50%)
  matrix products  343 us (24%)
  blocking collectives  172 us (12%)
  other arithmetic  77.3 us (6%)
  local copies, waits for them, and re-layouts  74 us (5%)
  between operations  25 us (2%)
    unnamed x18, waiting for transfers between devices  515 us
    psum x1, waiting for transfers between devices, per_device(): lax.psum((part_square, part_qkv, part_up, part_down, part_small), 'dp')  115 us
    psum x2, blocking collectives, per_device(): lax.psum((loss_local, jnp.sum(chosen_float)), ('fsdp', 'dp'))  98.3 us
    dot_general x15, matrix products, orthogonalize(): jnp.dot(poly_low, current, preferred_element_type=jnp.float32)  64.5 us
    dot_general x15, matrix products, orthogonalize(): jnp.dot(current, current.T, preferred_element_type=jnp.float32)  57.8 us
    unnamed x143, local copies, waits for them, and re-layouts  35.1 us
    all_gather x1, waiting for transfers between devices, per_device(): lax.all_gather(down_low, 'fsdp', axis=1, tiled=True)  31.9 us
    dot_general x1, matrix products, attend_backward(): jnp.einsum('hqk,khd->qhd', scores_low, key_rows, preferred_element_type=j...  31.7 us
  transfers between devices with their start and end apart: 13, of which 10 were waited for; matrix products, arithmetic and copies ran while one was open for 18% of the time, Pallas kernels for 0%

commit v1 on v0

v1 whole, which is shorter than its diff:
```python
from functools import partial
import math

import jax
import jax.numpy as jnp
import numpy as np
from jax import lax
from jax.experimental import pallas as pl
from jax.experimental.pallas import tpu as pltpu
from jax.sharding import PartitionSpec as P

D = 768
FF = 3072
HEADS = 12
HEAD_DIM = 64
GRID = 24
SHORT_GRID = 14
NS_ITERS = 5
STEP = 10
PATCHES = 576
SHORT_PATCHES = 196
UP_ROWS = FF // D
POS = SHORT_PATCHES + 1
SMALL_ROWS = 14 + UP_ROWS + POS
CLASS_ROW = PATCHES
TOKENS = 592
SMALL_PAD = 256
MIB = 1024 * 1024
SCALE = HEAD_DIM**-0.5

layer_eps = 1e-06
coeff_first, coeff_second, coeff_third = (3.4445, -4.775, 2.0315)
momentum_decay = 0.95
muon_rate = 0.15
muon_decay = 0.01
beta_first = 0.9
beta_second = 0.999
adam_rate = 0.3
adam_eps = 1e-08
clip_limit = 0.5
masked_score = -1000000000.0

BOTH = ("fsdp", "dp")
bfloat = jnp.bfloat16
float32 = jnp.float32


def interp_tables():
    axis_table = np.zeros((GRID, SHORT_GRID), np.float64)
    for target in range(GRID):
        source = (target + 0.5) * SHORT_GRID / GRID - 0.5
        source = min(max(source, 0.0), SHORT_GRID - 1.0)
        below = int(math.floor(source))
        above = min(below + 1, SHORT_GRID - 1)
        axis_table[target, below] += 1.0 - (source - below)
        axis_table[target, above] += source - below
    axis_table = axis_table.astype(np.float32)
    long_table = np.zeros((TOKENS, POS), np.float32)
    long_table[:PATCHES, 1:] = np.kron(axis_table, axis_table)
    long_table[CLASS_ROW, 0] = 1.0
    short_table = np.zeros((TOKENS, POS), np.float32)
    short_table[:SHORT_PATCHES, 1:] = np.eye(SHORT_PATCHES)
    short_table[CLASS_ROW, 0] = 1.0
    return long_table, short_table


def cost(flops, bytes_accessed, transcendentals):
    return pl.CostEstimate(
        flops=flops, bytes_accessed=bytes_accessed, transcendentals=0
    )


def dot_nt(left, right):
    return lax.dot_general(left, right, (((1,), (1,)), ((), ())), preferred_element_type=float32)


def dot_nn(left, right):
    return lax.dot_general(left, right, (((1,), (0,)), ((), ())), preferred_element_type=float32)


def dot_tn(left, right):
    return lax.dot_general(left, right, (((0,), (0,)), ((), ())), preferred_element_type=float32)


def attend_forward_kernel(q_ref, k_ref, v_ref, keep_ref, context_ref, logsum_ref):
    keep = keep_ref[...] > 0
    outs = []
    for head in range(2):
        cols = slice(HEAD_DIM * head, HEAD_DIM * (head + 1))
        query, key, value = q_ref[:, cols] * SCALE, k_ref[:, cols], v_ref[:, cols]
        scores = jnp.where(keep, dot_nt(key, query), masked_score)
        peak = jnp.max(scores, axis=0, keepdims=True)
        expo = jnp.exp(scores - peak)
        total = jnp.sum(expo, axis=0, keepdims=True)
        probs = (expo * (1.0 / total)).astype(bfloat)
        outs.append(dot_nn(value.T, probs).T.astype(bfloat))
        logsum_ref[head] = peak + jnp.log(total)
    context_ref[...] = jnp.concatenate(outs, axis=1)


def attend_backward_kernel(
    place_ref, q_ref, k_ref, v_ref, grad_ref, logsum_ref, keep_ref, mixed_ref, sums_ref
):
    keep = keep_ref[...] > 0
    grads_query, grads_key, grads_value = [], [], []
    for head in range(2):
        cols = slice(HEAD_DIM * head, HEAD_DIM * (head + 1))
        query, key, value, grad = q_ref[:, cols], k_ref[:, cols], v_ref[:, cols], grad_ref[:, cols]
        query, scaled_key = query * SCALE, key * SCALE
        scores = dot_nt(key, query)
        probs = jnp.where(keep, jnp.exp(scores - logsum_ref[head]), 0.0)
        grad_probs = dot_nt(value, grad)
        grads_value.append(dot_nn(probs.astype(bfloat), grad))
        mixed = probs * grad_probs
        total = jnp.sum(mixed, axis=0, keepdims=True)
        scores_low = (mixed - probs * total).astype(bfloat)
        grads_key.append(dot_nn(scores_low, query))
        grads_query.append(dot_nn(scaled_key.T, scores_low).T)
    grad_query = jnp.concatenate(grads_query, axis=1)
    grad_value = jnp.concatenate(grads_value, axis=1)
    mixed_ref[0] = grad_query.astype(bfloat)
    mixed_ref[1] = jnp.concatenate(grads_key, axis=1).astype(bfloat)
    mixed_ref[2] = grad_value.astype(bfloat)
    sums_ref[0:1, :] = jnp.sum(grad_query, axis=0, keepdims=True)
    sums_ref[1:2, :] = jnp.sum(grad_value, axis=0, keepdims=True)


def head_block(offset):
    return pl.BlockSpec((TOKENS, 2 * HEAD_DIM), lambda pair: (0, offset + pair))


KEEP_BLOCK = pl.BlockSpec((TOKENS, 1), lambda pair: (0, 0))
LOGSUM_BLOCK = pl.BlockSpec((2, 1, TOKENS), lambda pair: (pair, 0, 0))
PAIRS = HEADS // 2


def attend_forward(mixed, keep):
    return pl.pallas_call(
        attend_forward_kernel,
        grid=(PAIRS,),
        in_specs=[head_block(0), head_block(PAIRS), head_block(2 * PAIRS), KEEP_BLOCK],
        out_specs=[head_block(0), LOGSUM_BLOCK],
        out_shape=[
            jax.ShapeDtypeStruct((TOKENS, D), bfloat),
            jax.ShapeDtypeStruct((HEADS, 1, TOKENS), float32),
        ],
        cost_estimate=cost(
            flops=8 * TOKENS * TOKENS * D, bytes_accessed=8 * TOKENS * D, transcendentals=0
        ),
        compiler_params=pltpu.CompilerParams(vmem_limit_bytes=24 * MIB),
    )(mixed, mixed, mixed, keep)


def attend_backward(mixed, grad, logsum, keep, part, count):
    pairs = PAIRS // count
    lanes = 2 * HEAD_DIM

    def block(offset):
        return pl.BlockSpec((TOKENS, lanes), lambda pair, place: (0, offset + place[0] * pairs + pair))

    return pl.pallas_call(
        attend_backward_kernel,
        grid_spec=pltpu.PrefetchScalarGridSpec(
            num_scalar_prefetch=1,
            grid=(pairs,),
            in_specs=[
                block(0),
                block(PAIRS),
                block(2 * PAIRS),
                block(0),
                pl.BlockSpec((2, 1, TOKENS), lambda pair, place: (place[0] * pairs + pair, 0, 0)),
                pl.BlockSpec((TOKENS, 1), lambda pair, place: (0, 0)),
            ],
            out_specs=[
                pl.BlockSpec((3, TOKENS, lanes), lambda pair, place: (0, 0, pair)),
                pl.BlockSpec((2, lanes), lambda pair, place: (0, pair)),
            ],
        ),
        out_shape=[
            jax.ShapeDtypeStruct((3, TOKENS, pairs * lanes), bfloat),
            jax.ShapeDtypeStruct((2, pairs * lanes), float32),
        ],
        cost_estimate=cost(
            flops=20 * TOKENS * TOKENS * pairs * lanes,
            bytes_accessed=16 * TOKENS * pairs * lanes,
            transcendentals=0,
        ),
        compiler_params=pltpu.CompilerParams(vmem_limit_bytes=28 * MIB),
    )(part.reshape(1).astype(jnp.int32), mixed, mixed, mixed, grad, logsum, keep)


def stack_kernel(*refs):
    out_ref, start = refs[-1], 0
    for ref in refs[:-1]:
        out_ref[start : start + ref.shape[0], :] = ref[...]
        start += ref.shape[0]
    out_ref[start:, :] = jnp.zeros((out_ref.shape[0] - start, out_ref.shape[1]), out_ref.dtype)


def stacked_rows(parts, count):
    return pl.pallas_call(
        stack_kernel, out_shape=jax.ShapeDtypeStruct((count, parts[0].shape[1]), float32)
    )(*parts)


def gelu_parts(values):
    size = 1.0 + 0.23164189 * jnp.abs(values)
    inner = pl.reciprocal(size, approx=True)
    inner = inner * (2.0 - size * inner)
    poly = jnp.full_like(inner, 0.5 * 1.061405429)
    for coeff in (-1.453152027, 1.421413741, -0.284496736, 0.254829592):
        poly = poly * inner + 0.5 * coeff
    bell = jnp.exp(-0.5 * values * values)
    tail = poly * inner * bell
    below = jnp.where(values >= 0.0, 1.0 - tail, tail)
    return values * below, below + values * (0.3989422804014327 * bell)


UP_TILE = 768
UP_ROW_TILE = 160


def up_kernel(normed_ref, weight_ref, bias_ref, activ_ref, slope_ref):
    for start in range(0, TOKENS, UP_ROW_TILE):
        rows = slice(start, min(start + UP_ROW_TILE, TOKENS))
        hidden = dot_nn(normed_ref[rows], weight_ref[...]) + bias_ref[...]
        activ, slope = gelu_parts(hidden)
        activ_ref[rows] = activ.astype(bfloat)
        slope_ref[rows] = slope


def up_forward(normed, weight, bias):
    tile = pl.BlockSpec((TOKENS, UP_TILE), lambda step: (0, step))
    return pl.pallas_call(
        up_kernel,
        grid=(FF // UP_TILE,),
        in_specs=[
            pl.BlockSpec((TOKENS, D), lambda step: (0, 0)),
            pl.BlockSpec((D, UP_TILE), lambda step: (0, step)),
            pl.BlockSpec((1, UP_TILE), lambda step: (0, step)),
        ],
        out_specs=[tile, tile],
        out_shape=[
            jax.ShapeDtypeStruct((TOKENS, FF), bfloat),
            jax.ShapeDtypeStruct((TOKENS, FF), float32),
        ],
        cost_estimate=cost(
            flops=2 * TOKENS * D * FF, bytes_accessed=20 * MIB, transcendentals=0
        ),
        compiler_params=pltpu.CompilerParams(vmem_limit_bytes=20 * MIB),
    )(normed, weight, bias)


def hidden_kernel(branch_ref, weight_ref, slope_ref, hidden_ref, sums_ref):
    grad = dot_nn(branch_ref[...], weight_ref[...]) * slope_ref[...]
    hidden_ref[...] = grad.astype(bfloat)
    sums_ref[...] = jnp.sum(grad, axis=0, keepdims=True)


def hidden_backward(branch, weight, slope):
    tile = pl.BlockSpec((TOKENS, UP_TILE), lambda step: (0, step))
    return pl.pallas_call(
        hidden_kernel,
        grid=(FF // UP_TILE,),
        in_specs=[
            pl.BlockSpec((TOKENS, D), lambda step: (0, 0)),
            pl.BlockSpec((D, UP_TILE), lambda step: (0, step)),
            tile,
        ],
        out_specs=[tile, pl.BlockSpec((1, UP_TILE), lambda step: (0, step))],
        out_shape=[
            jax.ShapeDtypeStruct((TOKENS, FF), bfloat),
            jax.ShapeDtypeStruct((1, FF), float32),
        ],
        cost_estimate=cost(
            flops=2 * TOKENS * D * FF, bytes_accessed=20 * MIB, transcendentals=0
        ),
        compiler_params=pltpu.CompilerParams(vmem_limit_bytes=20 * MIB),
    )(branch, weight, slope)


def normalized(values):
    centred = values - jnp.mean(values, axis=-1, keepdims=True)
    variance = jnp.mean(centred * centred, axis=-1, keepdims=True)
    inverse = lax.rsqrt(variance + layer_eps)
    return centred * inverse, inverse


def norm_backward(grad, unit, inverse, gain):
    grad_unit = grad * gain
    mean_grad = jnp.mean(grad_unit, axis=-1, keepdims=True)
    mean_mixed = jnp.mean(grad_unit * unit, axis=-1, keepdims=True)
    grad_values = inverse * (grad_unit - mean_grad - unit * mean_mixed)
    return (
        grad_values,
        jnp.sum(grad * unit, axis=0, keepdims=True),
        jnp.sum(grad, axis=0, keepdims=True),
    )


TILE = 256


def ortho_kernel(squares_ref, own_ref, other_ref, out_ref, full_ref, gram_ref, poly_ref, *, places, shares, stride):
    rows, share = own_ref.shape[1], own_ref.shape[2]
    own_rows = out_ref.shape[0]
    width = shares * stride

    def pieces():
        for core, ref in enumerate((own_ref, other_ref)):
            for place in range(places):
                for part in range(2):
                    for column in range(shares):
                        index = place * shares + column if part == 0 else column * places + place
                        top = core * (D // 2) + (2 * place + part) * rows
                        yield ref, part * places * shares + index, top, column

    def inverse_norm(total):
        return 1.0 / (jnp.sqrt(total) + 1e-07)

    def mirrored(ref, make):
        for i in range(D // TILE):
            ref[i * TILE : (i + 1) * TILE, : (i + 1) * TILE] = make(i).astype(bfloat)
            for j in range(i):
                block = ref[i * TILE : (i + 1) * TILE, j * TILE : (j + 1) * TILE]
                ref[j * TILE : (j + 1) * TILE, i * TILE : (i + 1) * TILE] = block.T

    def grams(start, columns):
        def gram(i):
            return dot_nt(
                full_ref[i * TILE : (i + 1) * TILE, pl.ds(start, columns)],
                full_ref[: (i + 1) * TILE, pl.ds(start, columns)],
            )

        def poly(i):
            block = gram_ref[i * TILE : (i + 1) * TILE, :]
            product = dot_nn(block, gram_ref[:, : (i + 1) * TILE])
            return coeff_second * block[:, : (i + 1) * TILE].astype(float32) + coeff_third * product

        mirrored(gram_ref, gram)
        mirrored(poly_ref, poly)

    def step(start, columns, tall, target):
        old = full_ref[:, pl.ds(start, columns)]
        fresh = coeff_first * old[:tall].astype(float32) + dot_nn(poly_ref[:tall, :], old)
        target[:tall, pl.ds(start, columns)] = fresh.astype(bfloat)

    @pl.when(squares_ref[0] == 0)
    def one_matrix():
        total = jnp.zeros((), float32)
        for ref in (own_ref, other_ref):
            for index in range(ref.shape[0]):
                values = ref[index].astype(float32)
                total = total + jnp.sum(values * values)
        scale = inverse_norm(total)
        for ref, index, top, column in pieces():
            full_ref[top : top + rows, column * share : (column + 1) * share] = (
                ref[index].astype(float32) * scale
            ).astype(bfloat)
        columns = shares * share

        @pl.loop(0, NS_ITERS - 1)
        def sweep(index):
            grams(0, columns)
            step(0, columns, D, full_ref)

        grams(0, columns)
        step(0, columns, own_rows, out_ref)

    @pl.when(squares_ref[0] != 0)
    def three_matrices():
        for square in range(3):
            part = slice(square * stride, (square + 1) * stride)
            total = jnp.zeros((), float32)
            for ref in (own_ref, other_ref):
                for index in range(ref.shape[0]):
                    values = ref[index, :, part].astype(float32)
                    total = total + jnp.sum(values * values)
            scale = inverse_norm(total)
            for ref, index, top, column in pieces():
                left = square * width + column * stride
                full_ref[top : top + rows, left : left + stride] = (
                    ref[index, :, part].astype(float32) * scale
                ).astype(bfloat)

        @pl.loop(0, 3)
        def one(square):
            start = pl.multiple_of(square * width, 128)

            @pl.loop(0, NS_ITERS - 1)
            def sweep(index):
                grams(start, width)
                step(start, width, D, full_ref)

            grams(start, width)
            step(start, width, own_rows, out_ref)


def orthogonalize(squares, own, other, places, shares, stride, own_rows):
    count, rows, share = own.shape
    columns = max(shares * share, 3 * shares * stride)
    return pl.pallas_call(
        partial(ortho_kernel, places=places, shares=shares, stride=stride),
        in_specs=[
            pl.BlockSpec(memory_space=pltpu.SMEM),
            pl.BlockSpec(memory_space=pltpu.VMEM),
            pl.BlockSpec(memory_space=pltpu.VMEM),
        ],
        out_specs=pl.BlockSpec(memory_space=pltpu.VMEM),
        out_shape=jax.ShapeDtypeStruct((own_rows, columns), bfloat),
        scratch_shapes=[
            pltpu.VMEM((D, columns), bfloat),
            pltpu.VMEM((D, D), bfloat),
            pltpu.VMEM((D, D), bfloat),
        ],
        cost_estimate=cost(
            flops=10 * D * D * (2 * FF + D), bytes_accessed=8 * MIB, transcendentals=0
        ),
        compiler_params=pltpu.CompilerParams(vmem_limit_bytes=44 * MIB),
    )(squares, own, other)


class Wires:
    def __init__(self):
        self.fsdp_size, self.dp_size = lax.axis_size("fsdp"), lax.axis_size("dp")
        self.count = self.fsdp_size * self.dp_size
        self.fsdp, self.dp = lax.axis_index("fsdp"), lax.axis_index("dp")
        self.me = self.fsdp * self.dp_size + self.dp
        dp_bits = self.dp_size.bit_length() - 1
        all_bits = self.count.bit_length() - 1
        assert self.count == 1 << all_bits and self.fsdp_size >= 8
        self.dp_bits = list(range(dp_bits))
        self.core_bit = dp_bits
        self.row_bits = list(range(dp_bits + 1, all_bits - 2))
        self.near_bit, self.far_bit = all_bits - 2, all_bits - 1
        self.all_bits = list(range(all_bits))
        self.group = self.me >> self.near_bit

    def bit(self, bit):
        return (self.me >> bit) & 1

    def swap(self, values, bit):
        return self.swap_mask(values, 1 << bit)

    def swap_mask(self, values, mask):
        return lax.ppermute(values, BOTH, [(i, i ^ mask) for i in range(self.count)])

    def total(self, values):
        for bit in [self.core_bit] + self.dp_bits + self.row_bits + [self.near_bit, self.far_bit]:
            values = values + self.swap(values, bit)
        return values


def after(values, *others):
    return lax.optimization_barrier((values,) + others)[0]


def together(*values):
    return lax.optimization_barrier(values)


def split_exact(values):
    high = values.astype(bfloat)
    return jnp.concatenate([high, (values - high.astype(float32)).astype(bfloat)], axis=-1)


def joined_exact(sent):
    width = sent.shape[-1] // 2
    return sent[..., :width].astype(float32) + sent[..., width:].astype(float32)


def own_selection(wires):
    low = wires.fsdp_size // 4
    block = D // wires.fsdp_size
    place = jnp.arange(D // 2)
    distance, group, inner = place // (4 * block), place // block % 4, place % block
    count = len(wires.row_bits)
    flips = sum(
        ((distance >> (count - 1 - i)) & 1) << (bit - wires.core_bit)
        for i, bit in enumerate(wires.row_bits)
    )
    source = (group * low + ((wires.fsdp % low) ^ flips)) * block + inner
    return (source[:, None] == jnp.arange(D)[None, :]).astype(bfloat)


def pair_kernel(
    place_ref, select_ref, left_ref, left_other_ref, right_ref, right_other_ref,
    near_ref, away_ref, rows_ref, rows_other_ref, *, by_rows, halves
):
    @pl.when((pl.program_id(0) == 0) & (pl.program_id(1) == 0) & (pl.program_id(2) == 0))
    def select():
        rows_ref[...] = dot_nt(select_ref[...], left_ref[...]).astype(bfloat)
        rows_other_ref[...] = dot_nt(select_ref[...], left_other_ref[...]).astype(bfloat)

    right = right_ref[...].reshape(right_ref.shape[-2:])
    right_other = right_other_ref[...].reshape(right.shape)
    product = dot_nn(rows_ref[...], right) + dot_nn(rows_other_ref[...], right_other)
    if by_rows:
        half = product.shape[0] // 2
        near_ref[0, 0] = product[:half]
        away_ref[0, 0] = product[half:].astype(bfloat)
    else:

        @pl.when(pl.program_id(0) < halves)
        def away():
            away_ref[0, 0] = product.astype(bfloat)

        @pl.when(pl.program_id(0) >= halves)
        def near():
            near_ref[0, 0] = product


def column_tiles(width, cuts):
    sizes = [size for size in (768, 512, 384, 256, 128) if width % size == 0 and width // size >= cuts]
    return sizes[0] if sizes else width


def pair_grad(wires, select, left, right, by_rows, parts=None, cut=None):
    left, left_other = left
    right, right_other = right
    tokens, columns = right.shape[1:]
    first_part, parts = (0, right.shape[0]) if parts is None else parts
    dp_size = wires.dp_size
    width = columns // dp_size
    halves = dp_size // 2
    tile = column_tiles(width, 1 if cut is None else 2)
    all_steps = width // tile
    first_step, steps = 0, all_steps
    if cut is not None:
        edge = all_steps // 2
        first_step, steps = (0, edge) if cut == 0 else (edge, all_steps - edge)
    if tile % 128:
        right, right_other = (
            item.reshape(item.shape[0], tokens, dp_size, width).transpose(2, 0, 1, 3)
            for item in (right, right_other)
        )

    def distance(turn):
        return turn if by_rows else jnp.where(turn < halves, 2 * turn + 1, 2 * (turn - halves))

    def right_place(turn, part, step, place):
        column = distance(turn) ^ place[0]
        if right.ndim == 4:
            return (column, first_part + part, 0, 0)
        return (first_part + part, 0, column * all_steps + first_step + step)

    right_block = (1, 1, tokens, width) if right.ndim == 4 else (1, tokens, tile)
    rows = D // 2
    if by_rows:
        rows //= 2
        count = dp_size

        def near_place(turn, part, step, place):
            return (turn, part, 0, step)

        away_place = near_place
    else:
        count = halves

        def near_place(turn, part, step, place):
            there = turn >= halves
            return (
                jnp.maximum(turn - halves, 0),
                jnp.where(there, part, 0),
                0,
                jnp.where(there, step, 0),
            )

        def away_place(turn, part, step, place):
            there = turn < halves
            return (
                jnp.minimum(turn, halves - 1),
                jnp.where(there, part, parts - 1),
                0,
                jnp.where(there, step, steps - 1),
            )

    whole = pl.BlockSpec((tokens, D), lambda turn, part, step, place: (0, 0))
    shape = (count, parts, rows, steps * tile)
    return pl.pallas_call(
        partial(pair_kernel, by_rows=by_rows, halves=halves),
        grid_spec=pltpu.PrefetchScalarGridSpec(
            num_scalar_prefetch=1,
            grid=(dp_size, parts, steps),
            in_specs=[
                pl.BlockSpec((D // 2, D), lambda turn, part, step, place: (0, 0)),
                whole,
                whole,
                pl.BlockSpec(right_block, right_place),
                pl.BlockSpec(right_block, right_place),
            ],
            out_specs=[
                pl.BlockSpec((1, 1, rows, tile), near_place),
                pl.BlockSpec((1, 1, rows, tile), away_place),
            ],
            scratch_shapes=[pltpu.VMEM((D // 2, tokens), bfloat)] * 2,
        ),
        out_shape=[
            jax.ShapeDtypeStruct(shape, float32),
            jax.ShapeDtypeStruct(shape, bfloat),
        ],
        cost_estimate=cost(
            flops=2 * tokens * D * dp_size * steps * tile * parts,
            bytes_accessed=4 * D * dp_size * steps * tile * parts,
            transcendentals=0,
        ),
        compiler_params=pltpu.CompilerParams(vmem_limit_bytes=14 * MIB),
    )(wires.dp.reshape(1).astype(jnp.int32), select, left, left_other, right, right_other)


def product_kernel(select_ref, left_ref, left_other_ref, right_ref, right_other_ref, out_ref):
    rows = dot_nt(select_ref[...], left_ref[...]).astype(bfloat)
    rows_other = dot_nt(select_ref[...], left_other_ref[...]).astype(bfloat)
    width = right_ref.shape[-1]
    for part in range(right_ref.shape[0]):
        product = dot_nn(rows, right_ref[part]) + dot_nn(rows_other, right_other_ref[part])
        out_ref[:, part * width : (part + 1) * width] = product.astype(out_ref.dtype)


def pair_product(select, left, right, kind):
    parts, tokens, width = right[0].shape
    return pl.pallas_call(
        product_kernel,
        out_shape=jax.ShapeDtypeStruct((select.shape[0], parts * width), kind),
        cost_estimate=cost(
            flops=2 * tokens * D * parts * width, bytes_accessed=8 * MIB, transcendentals=0
        ),
        compiler_params=pltpu.CompilerParams(vmem_limit_bytes=16 * MIB),
    )(select, *left, *right)


def mixed_kernel(place_ref, away_ref, near_ref, weight_ref, out_ref):
    turn, part = pl.program_id(0), pl.program_id(1)

    @pl.when((turn == 0) & (part == 0))
    def start():
        out_ref[...] = jnp.zeros_like(out_ref)

    @pl.when(turn == 0)
    def away():
        out_ref[...] += dot_nt(away_ref[0], weight_ref[...])

    @pl.when(turn == 1)
    def near():
        out_ref[...] += dot_nt(near_ref[0], weight_ref[...])


def mixed_backward(place, away, near, weight):
    width = away.shape[-1]
    return pl.pallas_call(
        mixed_kernel,
        grid_spec=pltpu.PrefetchScalarGridSpec(
            num_scalar_prefetch=1,
            grid=(2, 3),
            in_specs=[
                pl.BlockSpec(
                    (1, TOKENS, width), lambda turn, part, place: (jnp.where(turn == 0, part, 2), 0, 0)
                ),
                pl.BlockSpec(
                    (1, TOKENS, width), lambda turn, part, place: (jnp.where(turn == 1, part, 0), 0, 0)
                ),
                pl.BlockSpec(
                    (D, width), lambda turn, part, place: (0, 2 * part + (place[0] ^ (1 - turn)))
                ),
            ],
            out_specs=pl.BlockSpec((TOKENS, D), lambda turn, part, place: (0, 0)),
        ),
        out_shape=jax.ShapeDtypeStruct((TOKENS, D), float32),
        cost_estimate=cost(
            flops=6 * TOKENS * D * D, bytes_accessed=10 * MIB, transcendentals=0
        ),
        compiler_params=pltpu.CompilerParams(vmem_limit_bytes=14 * MIB),
    )(place.reshape(1).astype(jnp.int32), away, near, weight)


def fold(values):
    distances, parts, rows, width = values.shape
    return values.transpose(0, 2, 1, 3).reshape(distances, rows, parts * width)


class Flow:
    def __init__(self, wires, plain, exact=None):
        self.wires, self.plain, self.exact, self.sent = wires, plain, exact, []

    @staticmethod
    def halves(values, by_rows):
        if by_rows:
            half = values.shape[1] // 2
            return values[:, :half], values[:, half:]
        values = values.reshape((values.shape[0] // 2, 2) + values.shape[1:])
        return values[:, 0], values[:, 1]

    def send(self, away, away_exact, bit):
        parts = [item.astype(bfloat) for item in away]
        if away_exact is not None:
            parts.append(split_exact(away_exact))
        self.sent.append(jnp.concatenate(parts, axis=-1) if len(parts) > 1 else parts[0])
        return self.wires.swap(self.sent[-1], bit)

    def halved(self, values, bit):
        return (None, None) if values is None else self.halves(values, bit in self.wires.row_bits)

    def finish(self, near, near_exact, got):
        start, sums = 0, []
        for item in near:
            width = item.shape[-1]
            sums.append(item + got[..., start : start + width].astype(float32))
            start += width
        exact = None if near_exact is None else near_exact + joined_exact(got[..., start:])
        return sums, exact

    def land(self, hold=()):
        pairs, near_exact, got = self.pending
        got = after(got, *hold) if hold else got
        self.plain, self.exact = self.finish([near for near, away in pairs], near_exact, got)
        return self

    def next(self, bit, hold=()):
        self.land(hold)
        by_rows = bit in self.wires.row_bits
        pairs = [self.halves(item, by_rows) for item in self.plain]
        near_exact, away_exact = self.halved(self.exact, bit)
        self.pending = (pairs, near_exact, self.send([away for near, away in pairs], away_exact, bit))
        return self

    def first(self, pairs, bit, exact=None):
        near_exact, away_exact = (
            (None, None) if exact is None else self.halves(exact, bit in self.wires.row_bits)
        )
        self.pending = (pairs, near_exact, self.send([away for near, away in pairs], away_exact, bit))
        return self


def gather_relative(wires, values, order):
    for bit in order:
        values = jnp.stack([values, wires.swap(values, bit)])
    return values


def dp_columns(wires, values):
    width = values.shape[-1] // wires.dp_size
    return lax.dynamic_slice_in_dim(values, wires.dp * width, width, values.ndim - 1)


def padded_to(values, width):
    pads = [(0, 0)] * (values.ndim - 1) + [(0, width - values.shape[-1])]
    return jnp.pad(values, pads)


def assemble_kernel(place_ref, *refs, pieces, count):
    outs, ins = refs[count:], refs[:count]
    row, core, dp = place_ref[0], place_ref[1], place_ref[2]
    for source, far_row, far_core, far_dp, start, matrix, offset, width in pieces:
        target = outs[matrix]
        part = target.shape[-1] // 2
        left = pl.multiple_of((dp ^ far_dp) * part + offset, 128)
        for group in range(4):
            target[group, row ^ far_row, core ^ far_core, :, pl.ds(left, width)] = ins[source[0]][
                source[1], group, :, start : start + width
            ]


def doubled(wires, values, bit, hold=()):
    got = wires.swap(values, bit)
    return jnp.stack([values, after(got, *hold) if hold else got])


def in_order(wires, values):
    return jnp.stack(
        [
            lax.dynamic_slice(
                values,
                ((group & 1) ^ wires.bit(wires.near_bit), (group >> 1) ^ wires.bit(wires.far_bit), 0, 0),
                (1, 1) + values.shape[2:],
            )[0, 0]
            for group in range(4)
        ]
    )


class Streams:
    def __init__(self, wires, along, widths, split):
        self.wires, self.widths, self.split = wires, widths, split
        edge = sum(widths[:-1]) + split
        self.first, self.last = along[..., :edge], along[..., edge:]

    def near(self, hold=()):
        wires = self.wires
        self.first = doubled(wires, self.first, wires.row_bits[0], hold)
        self.last = doubled(wires, self.last, wires.dp_bits[0], hold)

    def far(self, hold):
        self.first_far, self.last_far = together(self.first_far, self.last_far, *hold)[:2]

    def send_far(self):
        wires = self.wires
        self.first_far = wires.swap(self.first, wires.dp_bits[0])
        self.last_far = wires.swap(self.last, wires.row_bits[0])

    def finish(self):
        wires, widths, split = self.wires, self.widths, self.split
        block = self.first.shape[2]
        arrays = [
            jnp.concatenate([self.first, self.first_far]), jnp.concatenate([self.last, self.last_far])
        ]
        arrays += [wires.swap(item, wires.core_bit) for item in arrays]
        pieces = []
        for far_core in range(2):
            for far in range(2):
                for index in range(2):
                    start = 0
                    place = 2 * far + index
                    for matrix, width in enumerate(widths[:-1] + [split]):
                        source = (2 * far_core, place)
                        pieces.append((source, index, far_core, far, start, matrix, 0, width))
                        start += width
                    source = (2 * far_core + 1, place)
                    width = widths[-1] - split
                    pieces.append((source, far, far_core, index, 0, len(widths) - 1, split, width))
        place = jnp.stack(
            [wires.bit(wires.row_bits[0]), wires.bit(wires.core_bit), wires.bit(wires.dp_bits[0])]
        )
        wholes = pl.pallas_call(
            partial(assemble_kernel, pieces=pieces, count=len(arrays)),
            in_specs=[pl.BlockSpec(memory_space=pltpu.SMEM)]
            + [pl.BlockSpec(memory_space=pltpu.VMEM)] * len(arrays),
            out_specs=[pl.BlockSpec(memory_space=pltpu.VMEM)] * len(widths),
            out_shape=[
                jax.ShapeDtypeStruct((4, 2, 2, block, 2 * width), bfloat) for width in widths
            ],
            cost_estimate=cost(
                flops=0, bytes_accessed=4 * D * 2 * sum(widths), transcendentals=0
            ),
            compiler_params=pltpu.CompilerParams(vmem_limit_bytes=40 * MIB),
        )(place.astype(jnp.int32), *arrays)
        return [whole.reshape(D, whole.shape[-1]) for whole in wholes]


def side_by_side(parts, stride, width):
    return padded_to(jnp.concatenate([padded_to(part, stride) for part in parts], axis=-1), width)


def per_device(
    patches,
    masks,
    groups,
    w_square,
    w_qkv,
    w_up,
    w_down,
    small,
    muon_square,
    muon_qkv,
    muon_up,
    muon_down,
    adam_first,
    adam_second,
):
    wires = Wires()
    block = D // wires.fsdp_size
    dp_size = wires.dp_size

    long_image = groups[0] > 0
    patch_limit = jnp.where(long_image, PATCHES, SHORT_PATCHES)
    row = jnp.arange(TOKENS)
    chosen = jnp.pad(masks[0] > 0, (0, TOKENS - PATCHES)) & (row < patch_limit)
    chosen_float = chosen.astype(float32)[:, None]
    mask_local = jnp.sum(chosen_float)

    half = SMALL_PAD // 2
    used = -(-SMALL_ROWS // 2)
    small_low = small.astype(bfloat).T
    own_count = jnp.full((block, half - used), mask_local)
    high_count = jnp.floor(own_count / 256.0)
    lane = lax.broadcasted_iota(jnp.int32, own_count.shape, 1)
    spare = jnp.where(lane == 0, high_count, jnp.where(lane == 1, own_count - 256.0 * high_count, 0.0))
    spare = spare.astype(bfloat)
    small_rows = jnp.concatenate(
        [
            small_low[:, :used],
            spare,
            padded_to(small_low[:, used:], used),
            spare,
        ],
        axis=1,
    )
    square_low = w_square.astype(bfloat)
    down_rows = w_down.astype(bfloat).T
    groups_low = [
        [square_low[0], small_rows, w_qkv.astype(bfloat)],
        [square_low[1], w_up.astype(bfloat)],
        [square_low[2], down_rows],
    ]
    half_widths = [[shard.shape[1] // 2 for shard in shards] for shards in groups_low]
    staged = (
        dp_size == 2
        and len(wires.row_bits) == 1
        and not any(width % 128 for widths in half_widths for width in widths)
    )
    if staged:
        near_bit, far_bit = wires.near_bit, wires.far_bit

        def own_columns(shards):
            return jnp.concatenate([dp_columns(wires, shard) for shard in shards], axis=1)

        early_own, middle_own, late_own = [own_columns(shards) for shards in groups_low]
        early_own = doubled(wires, doubled(wires, early_own, far_bit), near_bit)
        early = Streams(wires, in_order(wires, early_own), half_widths[0], 256)
        middle_own = after(middle_own, early.first)
        early.near()
        early.send_far()
        middle_own = doubled(wires, middle_own, far_bit)
        early.far((middle_own,))
        embed_weight, small_whole, qkv_weight = early.finish()
        counts = small_whole.reshape(D, 2, half)[:, :, used : used + 2].astype(float32)
        mask_count = (256.0 * jnp.sum(counts[:, :, 0]) + jnp.sum(counts[:, :, 1])) / block
    else:
        (embed_weight, small_whole, qkv_weight), (out_weight, up_weight), (
            head_weight,
            down_weight,
        ) = [
            [lax.all_gather(shard, "fsdp", axis=0, tiled=True) for shard in shards]
            for shards in groups_low
        ]
        mask_count = wires.total(jnp.full((8, 128), mask_local))[0, 0]
    params_small = jnp.concatenate(
        [small_whole[:, :used], small_whole[:, half : half + SMALL_ROWS - used]], axis=1
    ).T.astype(float32)

    down_moment, down_master = muon_down.T, w_down.T
    stride = -(-D // dp_size // 128) * 128
    share = max(FF // dp_size, 3 * stride)
    def sub_columns(parts):
        return side_by_side([dp_columns(wires, item) for item in parts], stride, share)

    def thirds(values):
        return [values[:, index * D : (index + 1) * D] for index in range(3)]

    moment_parts = jnp.stack(
        [
            padded_to(dp_columns(wires, down_moment), share),
            sub_columns(thirds(muon_qkv)),
            sub_columns([muon_square[index] for index in range(3)]),
            padded_to(dp_columns(wires, muon_up), share),
        ]
    )
    if staged:
        moment_parts = after(moment_parts, embed_weight)

    def send_groups(blocks):
        mine = wires.group
        got = [lax.dynamic_index_in_dim(blocks, mine, 0, keepdims=False)]
        for step in (1, 2, 3):
            sent = lax.dynamic_index_in_dim(blocks, mine ^ step, 0, keepdims=False)
            got.append(wires.swap_mask(sent, step << wires.near_bit))
        return got

    def by_group(got):
        got = jnp.stack(got)
        return jnp.stack(
            [
                lax.dynamic_index_in_dim(got, group ^ wires.group, 0, keepdims=False)
                for group in range(4)
            ]
        )

    def across_groups(blocks):
        return by_group(send_groups(blocks))

    moments_got = send_groups(moment_parts)

    long_table, short_table = interp_tables()
    table = jnp.where(long_image, long_table, short_table)
    position = params_small[14 + UP_ROWS : SMALL_ROWS]
    pixels = jnp.pad(patches[0], ((0, TOKENS - PATCHES), (0, 0)))
    is_patch = (row < PATCHES)[:, None]
    is_class = (row == CLASS_ROW)[:, None]
    embedded = jnp.where(
        chosen[:, None], params_small[1], dot_nn(pixels, embed_weight) + params_small[0]
    )
    embedded = jnp.where(is_patch, embedded, jnp.where(is_class, params_small[2], 0.0))
    resid_first = embedded + jnp.dot(table, position, precision=lax.Precision.HIGHEST)
    if staged:
        middle_own = doubled(wires, middle_own, near_bit, (resid_first,))
        middle = Streams(wires, in_order(wires, middle_own), half_widths[1], 512)
        late_own = after(late_own, middle.first, middle.last)
    unit_first, inverse_first = normalized(resid_first)
    normed_first = (unit_first * params_small[3] + params_small[4]).astype(bfloat)
    qkv_bias = jnp.concatenate([params_small[12], jnp.zeros((D,), float32), params_small[13]])
    mixed = (dot_nn(normed_first, qkv_weight) + qkv_bias).astype(bfloat)
    pixels_both = (pixels, wires.swap(pixels, wires.core_bit))
    mixed, *pixels_both = together(mixed, *pixels_both)
    first_both = (normed_first, wires.swap(normed_first, wires.core_bit))
    keep = ((row < patch_limit) | (row == CLASS_ROW)).astype(float32)[:, None]
    if staged:
        late_own = doubled(wires, late_own, far_bit, (mixed,))
        middle.near((mixed,))
        mixed = after(mixed, middle.first, middle.last, late_own)
        middle.send_far()
    context_low, logsum = attend_forward(mixed, keep)
    context_low, *first_both = together(context_low, *first_both)
    if staged:
        late_own = doubled(wires, late_own, near_bit, (context_low,))
        late = Streams(wires, in_order(wires, late_own), half_widths[2], 512)
        middle.far((context_low, late.first))
        out_weight, up_weight = middle.finish()
    context_both = (context_low, wires.swap(context_low, wires.core_bit))
    resid_second = resid_first + dot_nn(context_low, out_weight) + params_small[5]
    unit_second, inverse_second = normalized(resid_second)
    normed_second = (unit_second * params_small[6] + params_small[7]).astype(bfloat)
    up_bias = params_small[14 : 14 + UP_ROWS].reshape(-1)
    if staged:
        late.near((normed_second,))
        normed_second = after(normed_second, late.first, late.last)
        late.send_far()
    second_both = (normed_second, wires.swap(normed_second, wires.core_bit))
    activ_low, slope = up_forward(normed_second, up_weight, up_bias[None])
    activ_low, moments_got[1], context_other, second_other = together(
        activ_low, moments_got[1], context_both[1], second_both[1]
    )
    context_both, second_both = (context_low, context_other), (normed_second, second_other)
    if staged:
        late.far((activ_low,))
        head_weight, down_weight = late.finish()
    activ_both = (activ_low[None], wires.swap(activ_low, wires.core_bit)[None])
    resid_third = resid_second + dot_nt(activ_low, down_weight) + params_small[8]
    unit_final, inverse_final = normalized(resid_third)
    normed_final = (unit_final * params_small[9] + params_small[10]).astype(bfloat)
    predicted = dot_nn(normed_final, head_weight) + params_small[11]
    residual_error = predicted - pixels.astype(float32)
    loss_local = jnp.sum(chosen_float * residual_error * residual_error)

    core = wires.core_bit
    select = own_selection(wires)

    def other(values):
        return wires.swap(values, core)

    x_order = wires.dp_bits + wires.row_bits
    y_order = wires.row_bits + wires.dp_bits

    def both(values):
        return values, other(values)

    def both(values):
        return values, other(values)

    part_width = D // dp_size

    def blocks(values):
        return values.reshape(4, block, values.shape[-1])

    def wide_part(flows):
        return jnp.concatenate([blocks(item.plain[0]) for item in flows], axis=-1)

    def extra_part(flows):
        return blocks(next(item.plain[1] for item in flows if len(item.plain) > 1))

    near, far = wires.bit(wires.near_bit), wires.bit(wires.far_bit)

    def pick(flag, first, second):
        return jnp.where(flag == 0, first, second)

    class near_stage:
        def __init__(self, first, second, exact=None):
            self.keep, self.exact = pick(near, first, second), None
            parts = [pick(near, second, first).astype(bfloat)]
            if exact is not None:
                self.exact = pick(near, *exact)
                parts.append(split_exact(pick(near, exact[1], exact[0])))
            self.sent = jnp.concatenate(parts, axis=-1)
            self.got = wires.swap(self.sent, wires.near_bit)

        def land(self, hold=()):
            got = after(self.got, *hold) if hold else self.got
            width = self.keep.shape[-1]
            total = self.keep + got[..., :width].astype(float32)
            if self.exact is None:
                return total, None
            return total, self.exact + joined_exact(got[..., width:])

    def flow(pairs, order, exact=None):
        return Flow(wires, None).first(
            [(fold(near), fold(away)) for near, away in pairs], order[0], exact
        )

    def onward(flows, orders, hold=()):
        for item, order in zip(flows, orders):
            for bit in order[1:]:
                item.next(bit, hold)
        return [item.sent[-1] for item in flows]

    grad_pred = 2.0 / mask_count * chosen_float * residual_error
    pred_low = grad_pred.astype(bfloat)
    head_pair = pair_grad(wires, select, both(normed_final), both(pred_low[None]), False)
    grad_head_bias = jnp.sum(grad_pred, axis=0, keepdims=True)
    grad_normed = dot_nt(pred_low, head_weight)
    grad_resid, gain_final, shift_final = norm_backward(
        grad_normed, unit_final, inverse_final, params_small[9]
    )
    branch_low = grad_resid.astype(bfloat)
    branch_both = both(branch_low)
    down_pairs = [
        pair_grad(wires, select, branch_both, activ_both, cut == 1, cut=cut) for cut in range(2)
    ]
    down_flows = [flow([down_pairs[0], head_pair], x_order), flow(down_pairs[1:], y_order)]
    grad_down_bias = jnp.sum(grad_resid, axis=0, keepdims=True)
    hidden_low, grad_up_bias = hidden_backward(
        after(branch_low, *(item.sent[0] for item in down_flows)), down_weight, slope
    )
    hidden_both = both(hidden_low[None])
    grad_normed = dot_nt(hidden_low, up_weight)
    grad_part, gain_second, shift_second = norm_backward(
        grad_normed, unit_second, inverse_second, params_small[6]
    )
    grad_resid = grad_resid + grad_part
    branch_low = grad_resid.astype(bfloat)
    normed_both = second_both
    up_first = pair_grad(
        wires, select, normed_both, (after(hidden_both[0], branch_low), hidden_both[1]), False, cut=0
    )
    up_last = pair_grad(
        wires, select, normed_both, (after(hidden_both[0], up_first[1]), hidden_both[1]), True, cut=1
    )
    out_pair = pair_grad(
        wires, select, context_both, (after(branch_low, up_last[1])[None], other(branch_low)[None]),
        True,
    )
    up_flows = [flow([up_first], x_order), flow([up_last, out_pair], y_order)]
    grad_out_bias = jnp.sum(grad_resid, axis=0, keepdims=True)
    grad_context = dot_nt(after(branch_low, out_pair[1]), out_weight).astype(bfloat)
    sent = onward(down_flows, [x_order, y_order], (grad_context,))
    grad_context = after(grad_context, *sent, *(item.sent[-1] for item in up_flows))
    normed_both = first_both
    if dp_size == 2:
        away_low, away_sums = attend_backward(mixed, grad_context, logsum, keep, 1 - wires.dp, 2)
        away_both = both(away_low)
        for item in down_flows:
            item.land((away_low,))
        sent = onward(up_flows, [x_order, y_order], (away_low, *(item.plain[0] for item in down_flows)))
        away_pair = pair_product(
            select, normed_both, (after(away_both[0], *sent), away_both[1]), bfloat
        )
        grad_context = after(grad_context, away_pair)
        near_low, near_sums = attend_backward(mixed, grad_context, logsum, keep, wires.dp, 2)
        near_both = both(near_low)
        near_pair = pair_product(select, normed_both, near_both, float32)
        qkv_flow = Flow(wires, None).first([(near_pair[None], away_pair[None])], x_order[0])
        grad_normed = mixed_backward(wires.dp, away_low, after(near_low, near_pair), qkv_weight)
        for item in up_flows:
            item.land((grad_normed,))
        wide_near = near_stage(wide_part(down_flows), wide_part(up_flows))
        grad_normed = after(grad_normed, wide_near.sent)
        bias_sums = jnp.where(
            wires.dp == 0,
            jnp.concatenate([near_sums, away_sums], axis=1),
            jnp.concatenate([away_sums, near_sums], axis=1),
        )
    else:
        mixed_low, bias_sums = attend_backward(
            mixed, grad_context, logsum, keep, jnp.zeros((), jnp.int32), 1
        )
        for item in down_flows:
            item.land((mixed_low,))
        sent = onward(up_flows, [x_order, y_order], (mixed_low,))
        qkv_pair = pair_grad(wires, select, normed_both, both(mixed_low), False)
        qkv_flow = flow([qkv_pair], x_order)
        for item in up_flows:
            item.land()
        wide_near = near_stage(wide_part(down_flows), wide_part(up_flows))
        grad_normed = sum(dot_nt(mixed_low[i], thirds(qkv_weight)[i]) for i in range(3))
    grad_part, gain_first, shift_first = norm_backward(
        grad_normed, unit_first, inverse_first, params_small[3]
    )
    grad_resid = grad_resid + grad_part
    unchosen = jnp.where(is_patch & ~chosen[:, None], grad_resid, 0.0)
    unchosen_low = unchosen.astype(bfloat)
    unchosen_both = both(unchosen_low[None])
    sent = onward([qkv_flow], [x_order], (unchosen_low,))
    grad_resid = after(grad_resid, *sent)
    grad_leading = grad_resid[CLASS_ROW : CLASS_ROW + 1]
    grad_position = lax.dot_general(
        table, grad_resid, (((0,), (0,)), ((), ())), precision=lax.Precision.HIGHEST
    )
    grad_mask_token = jnp.sum(jnp.where(chosen[:, None], grad_resid, 0.0), axis=0, keepdims=True)
    grad_patch_bias = jnp.sum(unchosen, axis=0, keepdims=True)
    small_parts = [
        grad_patch_bias,
        grad_mask_token,
        grad_leading,
        gain_first,
        shift_first,
        grad_out_bias,
        gain_second,
        shift_second,
        grad_down_bias,
        gain_final,
        shift_final,
        grad_head_bias,
        bias_sums,
        grad_up_bias.reshape(UP_ROWS, D),
        grad_position,
    ]
    small_parts[-1] = after(grad_position, unchosen_both[1])
    grad_small = stacked_rows(small_parts, SMALL_PAD)

    wide_half, unused = wide_near.land((grad_small,))
    wide_far = wide_half.astype(bfloat)
    far_mask = 1 << wires.far_bit
    places = [((i >> wires.near_bit) & 1, (i >> wires.far_bit) & 1, i) for i in range(wires.count)]
    wide_got = lax.ppermute(
        wide_far, BOTH, [(i, i ^ far_mask) for n, f, i in places if n != f]
    )
    unchosen_both = (after(unchosen_both[0], wide_far), unchosen_both[1])
    patch_pair = pair_grad(wires, select, pixels_both, unchosen_both, False)

    tail = half // dp_size
    grad_small = grad_small + other(grad_small)
    grad_small = grad_small.reshape(2, dp_size, tail, D)
    grad_small = jnp.stack(
        [
            lax.dynamic_index_in_dim(grad_small, wires.dp ^ distance, 1, keepdims=False)
            for distance in range(dp_size)
        ]
    ).reshape(SMALL_PAD, D)
    layers, rest = [], grad_small
    for layer in range(3):
        layers.append(rest.astype(bfloat))
        rest = rest - layers[-1].astype(float32)
    small_own = sum(dot_nt(select, layer) for layer in layers)
    small_own = small_own.reshape(D // 2, dp_size, 2 * tail).transpose(1, 0, 2)
    patch_flow = flow([patch_pair], x_order, small_own)
    qkv_flow.land((patch_flow.sent[0],))
    onward([patch_flow], [x_order], (moments_got[2], *qkv_flow.plain))
    patch_flow.land((moments_got[3],))

    qkv_part = blocks(qkv_flow.plain[0])
    square_part = jnp.concatenate(
        [blocks(patch_flow.plain[0]), extra_part(up_flows), extra_part(down_flows)], axis=-1
    )
    small_part = blocks(patch_flow.exact)
    small_low_part, small_high_part = small_part[..., :tail], small_part[..., tail:]
    wide_sum = wide_half + after(wide_got, *patch_flow.sent).astype(float32)
    narrow_sum, small_sum = near_stage(
        after(square_part, wide_sum), qkv_part, (small_low_part, small_high_part)
    ).land()
    narrow_got = lax.ppermute(
        jnp.concatenate([narrow_sum.astype(bfloat), split_exact(small_sum)], axis=-1),
        BOTH,
        [(i, i ^ far_mask) for n, f, i in places if n == f],
    )
    narrow_sum = narrow_sum + narrow_got[..., : 3 * part_width].astype(float32)
    small_sum = small_sum + joined_exact(narrow_got[..., 3 * part_width :])
    narrow_sum = side_by_side(
        [narrow_sum[..., i * part_width : (i + 1) * part_width] for i in range(3)], stride, share
    )
    outer = near ^ far
    own_grad = pick(outer, padded_to(wide_sum, share), narrow_sum)
    own_small = pick(outer, jnp.zeros_like(small_sum), small_sum)
    own_grad, own_small = lax.optimization_barrier((own_grad, own_small))


    squares_local = jnp.sum(own_grad * own_grad) + jnp.sum(own_small * own_small)
    lane = lax.broadcasted_iota(jnp.int32, (8, 128), 1)
    scalars = wires.total(jnp.where(lane == 0, loss_local, squares_local))
    loss_sum = scalars[0, 0]
    grad_norm = jnp.sqrt(scalars[0, 1])
    factor = jnp.minimum(1.0, clip_limit / (grad_norm + 1e-06))

    own_moment = by_group(moments_got)
    grad_blocks = jnp.concatenate([own_grad.astype(bfloat), split_exact(own_small)], axis=-1)
    grad_blocks = after(grad_blocks, factor)
    grads_got = send_groups(grad_blocks)
    clipped = own_grad * factor
    blend = clipped + momentum_decay * (momentum_decay * own_moment + clipped)
    blend_low = blend.astype(bfloat)
    half_rows = 2 * block
    dps, rows = wires.dp_bits, wires.row_bits
    upper, lower = blend_low[:2].reshape(half_rows, share), blend_low[2:].reshape(half_rows, share)
    orders = list(zip(dps + rows, rows + dps))
    for turn, (upper_bit, lower_bit) in enumerate(orders):
        upper_got, lower_got = wires.swap(upper, upper_bit), wires.swap(lower, lower_bit)
        if turn < 2:
            upper_got, lower_got, grads_got[turn + 1] = together(
                upper_got, lower_got, grads_got[turn + 1]
            )
        upper, lower = jnp.stack([upper, upper_got]), jnp.stack([lower, lower_got])
    own_pieces = jnp.concatenate(
        [upper.reshape(-1, half_rows, share), lower.reshape(-1, half_rows, share)]
    )
    other_pieces = other(own_pieces)
    other_pieces, grads_got[3] = together(other_pieces, grads_got[3])
    grad_rows = by_group(grads_got)
    grad_all = gather_relative(wires, grad_rows, dps).reshape((dp_size,) + grad_rows.shape)
    own_pieces = after(own_pieces, grad_rows)
    squares_flag = (wires.group == 2).astype(jnp.int32).reshape(1)
    ortho = orthogonalize(
        squares_flag, own_pieces, other_pieces, 1 << len(rows), dp_size, stride, 4 * block
    )

    updates_got = send_groups(ortho.reshape(4, block, ortho.shape[1]))

    def joined(parts):
        parts = jnp.stack(parts)
        return jnp.concatenate(
            [
                lax.dynamic_index_in_dim(parts, place ^ wires.dp, 0, keepdims=False)
                for place in range(dp_size)
            ],
            axis=-1,
        ).astype(float32)

    def grad_columns(task, start, width):
        part = width // dp_size
        return joined([grad_all[far, task, :, start : start + part] for far in range(dp_size)])

    def update_columns(task, start, width, spread):
        part = width // dp_size
        return joined(
            [
                updates[task, :, far * spread + start : far * spread + start + part]
                for far in range(dp_size)
            ]
        )

    def three_grads(task):
        return [grad_columns(task, index * stride, D) for index in range(3)]

    grads = [
        jnp.stack(three_grads(2)),
        jnp.concatenate(three_grads(1), axis=1),
        grad_columns(3, 0, FF),
        grad_columns(0, 0, FF),
    ]
    olds = [muon_square, muon_qkv, muon_up, down_moment]
    masters = [w_square, w_qkv, w_up, down_master]
    new_moments = [
        momentum_decay * old + factor * fresh for old, fresh in zip(olds, grads)
    ]
    small_grad = jnp.concatenate(
        [
            grad_columns(task, share, half) + grad_columns(task, share + tail, half)
            for task in (2, 1)
        ],
        axis=1,
    )[:, :SMALL_ROWS].T
    small_grad = small_grad * factor
    new_first = beta_first * adam_first + (1.0 - beta_first) * small_grad
    new_second = beta_second * adam_second + (1.0 - beta_second) * small_grad * small_grad
    first_hat = new_first / (1.0 - beta_first**STEP)
    second_hat = new_second / (1.0 - beta_second**STEP)
    new_small = small - adam_rate * first_hat / (jnp.sqrt(second_hat) + adam_eps)
    early_outs = (*new_moments, new_small, new_first, new_second)
    updates_got, early_outs = lax.optimization_barrier((updates_got, early_outs))
    *new_moments, new_small, new_first, new_second = early_outs
    updates = by_group(updates_got)
    ups = [
        jnp.stack([update_columns(2, index * dp_size * stride, D, stride) for index in range(3)]),
        jnp.concatenate(
            [update_columns(1, index * stride, D, share) for index in range(3)], axis=1
        ),
        update_columns(3, 0, FF, share),
        update_columns(0, 0, FF, share),
    ]
    new_weights = [
        master * (1.0 - muon_rate * muon_decay)
        - muon_rate * 0.2 * math.sqrt(master.shape[-1]) * update
        for master, update in zip(masters, ups)
    ]
    return (
        loss_sum,
        mask_count,
        grad_norm,
        new_weights[0],
        new_moments[0],
        new_weights[1],
        new_moments[1],
        new_weights[2],
        new_moments[2],
        new_weights[3].T,
        new_moments[3].T,
        new_small,
        new_first,
        new_second,
    )


def solution(mesh):
    placed = (
        P(("fsdp", "dp"), None, None),
        P(("fsdp", "dp"), None),
        P(("fsdp", "dp")),
        P(None, "fsdp", None),
        P("fsdp", None),
        P("fsdp", None),
        P(None, "fsdp"),
        P(None, "fsdp"),
        P(None, "fsdp", None),
        P("fsdp", None),
        P("fsdp", None),
        P(None, "fsdp"),
        P(None, "fsdp"),
        P(None, "fsdp"),
    )
    return jax.shard_map(
        per_device,
        mesh=mesh,
        in_specs=placed,
        out_specs=(
            P(),
            P(),
            P(),
            P(None, "fsdp", None),
            P(None, "fsdp", None),
            P("fsdp", None),
            P("fsdp", None),
            P("fsdp", None),
            P("fsdp", None),
            P(None, "fsdp"),
            P(None, "fsdp"),
            P(None, "fsdp"),
            P(None, "fsdp"),
            P(None, "fsdp"),
        ),
        check_vma=False,
    )
```

time: 1400 us -> 538 us (0.38)
  waiting for transfers between devices: 698 us -> 158 us
  matrix products: 343 us -> 25.5 us
  blocking collectives: 172 us -> 0 us
  Pallas kernels: 0 us -> 144 us
  starting transfers between devices: 1.17 us -> 65.6 us
  local copies, waits for them, and re-layouts: 74 us -> 54.4 us
    unnamed x18 -> x0, waiting for transfers between devices: 515 us -> none
    dot_general x67 -> x13, matrix products: 316 us -> 25.5 us  [the longest x7 13.5 us: dot_nt(): lax.dot_general(left, right, (((1,), (1,)), ((), ())), preferred_element_...]
    ppermute x0 -> x74, waiting for transfers between devices: none -> 158 us  [the longest x72 145 us: swap_mask(): lax.ppermute(values, BOTH, [(i, i ^ mask) for i in range(self.count)])]
    pallas_call x0 -> x20, Pallas kernels: none -> 144 us  [the longest x1 37.6 us: orthogonalize(): pl.pallas_call(partial(ortho_kernel, places=places, shares=shares, stride...]
    psum x4 -> x0, blocking collectives: 129 us -> none  [the longest x2 98.3 us: per_device(): lax.psum((loss_local, jnp.sum(chosen_float)), ('fsdp', 'dp'))]
    psum x1 -> x0, waiting for transfers between devices: 115 us -> none  [per_device(): lax.psum((part_square, part_qkv, part_up, part_down, part_small), 'dp')]
    all_gather x7 -> x0, waiting for transfers between devices: 68 us -> none  [the longest x1 31.9 us: per_device(): lax.all_gather(down_low, 'fsdp', axis=1, tiled=True)]
    ppermute x0 -> x74, starting transfers between devices: none -> 65.6 us  [the longest x72 60.2 us: swap_mask(): lax.ppermute(values, BOTH, [(i, i ^ mask) for i in range(self.count)])]
  transfers between devices with their start and end apart: 13 -> 74, of which waited for: 10 -> 34; matrix products, arithmetic and copies ran while one was open for 18% -> 18% of each run, Pallas kernels for 0% -> 21%
where the time goes in v1:
time: 538 us; the launch traced here: 529 us
  waiting for transfers between devices  158 us (29%)
  Pallas kernels  144 us (27%)
  other arithmetic  71.2 us (13%)
  starting transfers between devices  65.6 us (12%)
  local copies, waits for them, and re-layouts  54.4 us (10%)
  matrix products  25.5 us (5%)
  between operations  11.3 us (2%)
    ppermute x72, waiting for transfers between devices, swap_mask(): lax.ppermute(values, BOTH, [(i, i ^ mask) for i in range(self.count)])  145 us
    ppermute x72, starting transfers between devices, swap_mask(): lax.ppermute(values, BOTH, [(i, i ^ mask) for i in range(self.count)])  60.2 us
    pallas_call x1, Pallas kernels, orthogonalize(): pl.pallas_call(partial(ortho_kernel, places=places, shares=shares, stride...  37.6 us
    pallas_call x7, Pallas kernels, pair_grad(): pl.pallas_call(partial(pair_kernel, by_rows=by_rows, halves=halves), grid...  35.5 us
    unnamed x264, local copies, waits for them, and re-layouts  29.7 us
    pallas_call x2, Pallas kernels, attend_backward(): pl.pallas_call(attend_backward_kernel, grid_spec=pltpu.PrefetchScalarGrid...  19.4 us
    dot_general x7, matrix products, dot_nt(): lax.dot_general(left, right, (((1,), (1,)), ((), ())), preferred_element_...  13.5 us
    pallas_call x1, Pallas kernels, attend_forward(): pl.pallas_call(attend_forward_kernel, grid=(PAIRS,), in_specs=[head_block...  13.1 us
  transfers between devices with their start and end apart: 74, of which 34 were waited for; matrix products, arithmetic and copies ran while one was open for 18% of the time, Pallas kernels for 21%

profile of v1, /device:TPU:20, one launch (start us, length us, event | category | flops | bytes accessed | tf_op | source)
XLA Modules:
  0.0 529.3 jit_solution(7754518935503030678)
XLA Ops:
  8.0 6.8 %collective-permute-done = bf16[48,1664]{1,0:T(8,128)(2,1)S(1)} collective-permute-done((bf16[48,1664]{1,0:T(8,128)(2,1)S(1)}, bf16[48,1664]{1,0:T(8,128)(2,1)S(1)}, u32[]{:S(2)}, u32[]{:S(2)}) %collective-permute-start) | collective-permute-done | bytes 159776 | tf_op jit(solution)/shard_map/ppermute | solution.py:446
  20.4 6.7 %collective-permute-done.1 = bf16[2,48,1664]{2,1,0:T(8,128)(2,1)S(1)} collective-permute-done((bf16[2,48,1664]{2,1,0:T(8,128)(2,1)S(1)}, bf16[2,48,1664]{2,1,0:T(8,128)(2,1)S(1)}, u32[]{:S(2)}, u32[]{:S(2)}) %collective-permute-start.1) | collective-permute-done | bytes 319520 | tf_op jit(solution)/shard_map/ppermute | solution.py:446
  29.8 7.3 %collective-permute-done.4 = bf16[4,48,896]{2,1,0:T(8,128)(2,1)S(1)} collective-permute-done((bf16[4,48,896]{2,1,0:T(8,128)(2,1)S(1)}, bf16[4,48,896]{2,1,0:T(8,128)(2,1)S(1)}, u32[]{:S(2)}, u32[]{:S(2)}) %collective-permute-start.4) | collective-permute-done | bytes 344096 | tf_op jit(solution)/shard_map/ppermute | solution.py:446
  89.6 13.1 %shard_map.264 = (bf16[592,768]{1,0:T(8,128)(2,1)}, f32[12,1,592]{2,1,0:T(1,128)S(1)}) custom-call(bf16[592,2304]{1,0:T(8,128)(2,1)S(1)} %add_convert_fusion.q_ref.k_ref.v_ref, bf16[592,2304]{1,0:T(8,128)(2,1)S(1)} %add_convert_fusion.q_ref.k_ref.v_ref, bf16[592,2304]{1,0:T(8,128)(2,1)S(1)} %add_convert_fusion.q_ref.k_ref.v_ref, f32[592,1]{1,0:T(8,128)S(1)} %fusion.20.keep_ref), custom_call_target="tpu_custom_call" | custom-call | flops 2153250816 | bytes 3637248 | tf_op jit(solution)/shard_map/pallas_call | solution.py:138
  132.1 11.0 %shard_map.266 = (bf16[592,3072]{1,0:T(8,128)(2,1)S(1)}, f32[592,3072]{1,0:T(8,128)S(1)}) custom-call(bf16[592,768]{1,0:T(8,128)(2,1)} %add_convert_fusion.2.normed_ref.left_ref, bf16[768,3072]{1,0:T(8,128)(2,1)S(1)} %bitcast.447, f32[1,3072]{1,0:T(1,128)S(1)} %bitcast.446), custom_call_target="tpu_custom_call" | custom-call | flops 2793406464 | bytes 20971520 | tf_op jit(solution)/shard_map/pallas_call | solution.py:234
  179.7 5.6 %shard_map.268 = (f32[1,1,384,768]{3,2,1,0:T(8,128)S(1)}, bf16[1,1,384,768]{3,2,1,0:T(8,128)(2,1)S(1)}) custom-call(s32[1]{0:T(128)} %bitcast.63.place_ref, bf16[384,768]{1,0:T(8,128)(2,1)S(1)} %fusion.8.select_ref, bf16[592,768]{1,0:T(8,128)(2,1)} %convert_element_type.408.left_ref.branch_ref, bf16[592,768]{1,0:T(8,128)(2,1)} %collective-permute-done.29.left_other_ref, ...), custom_call_target="tpu_custom_call" | custom-call | flops 1396703232 | bytes 4718592 | tf_op jit(solution)/shard_map/pallas_call | solution.py:580
  187.3 5.5 %shard_map.270 = (f32[2,1,192,768]{3,2,1,0:T(8,128)S(1)}, bf16[2,1,192,768]{3,2,1,0:T(8,128)(2,1)S(1)}) custom-call(s32[1]{0:T(128)} %bitcast.63.place_ref, bf16[384,768]{1,0:T(8,128)(2,1)S(1)} %fusion.8.select_ref, bf16[592,768]{1,0:T(8,128)(2,1)} %convert_element_type.408.left_ref.branch_ref, bf16[592,768]{1,0:T(8,128)(2,1)} %collective-permute-done.29.left_other_ref, ...), custom_call_target="tpu_custom_call" | custom-call | flops 1396703232 | bytes 4718592 | tf_op jit(solution)/shard_map/pallas_call | solution.py:580
  194.7 6.5 %shard_map.271 = (bf16[592,3072]{1,0:T(8,128)(2,1)}, f32[1,3072]{1,0:T(1,128)S(1)}) custom-call(bf16[592,768]{1,0:T(8,128)(2,1)} %convert_element_type.408.left_ref.branch_ref, bf16[768,3072]{1,0:T(8,128)(2,1)S(1)} %bitcast.432, f32[592,3072]{1,0:T(8,128)S(1)} %bitcast.428), custom_call_target="tpu_custom_call" | custom-call | flops 2793406464 | bytes 20971520 | tf_op jit(solution)/shard_map/pallas_call | solution.py:262
  201.8 5.5 %multiply_reduce_fusion.1 = (f32[768]{0:T(1024)S(1)}, f32[592]{0:T(1024)S(1)}, f32[592]{0:T(1024)S(1)}, f32[768]{0:T(1024)S(1)}, f32[592,768]{1,0:T(8,128)S(1)}) fusion(f32[592,768]{1,0:T(8,128)S(1)} %copy-done.40, f32[592]{0:T(1024)S(1)} %copy-done.114, f32[592]{0:T(1024)S(1)} %copy-done.104, f32[768]{0:T(1024)S(1)} %copy-done.112, ...), kind=kOutput, calls=%fused_computation.5 | convolution fusion | flops 2797495808 | bytes 12011776 | tf_op jit(solution)/shard_map/dot_general | solution.py:74
  212.4 5.4 %shard_map.272 = (f32[1,1,384,768]{3,2,1,0:T(8,128)S(1)}, bf16[1,1,384,768]{3,2,1,0:T(8,128)(2,1)S(1)}) custom-call(s32[1]{0:T(128)} %bitcast.63.place_ref, bf16[384,768]{1,0:T(8,128)(2,1)S(1)} %fusion.8.select_ref, bf16[592,768]{1,0:T(8,128)(2,1)} %add_convert_fusion.2.normed_ref.left_ref, bf16[592,768]{1,0:T(8,128)(2,1)} %collective-permute-done.24.left_other_ref, ...), custom_call_target="tpu_custom_call" | custom-call | flops 1396703232 | bytes 4718592 | tf_op jit(solution)/shard_map/pallas_call | solution.py:580
  238.5 9.2 %shard_map.275 = (bf16[3,592,384]{2,1,0:T(8,128)(2,1)S(1)}, f32[2,384]{1,0:T(2,128)S(1)}) custom-call(s32[1]{0:T(128)} %bitcast.75.place_ref, bf16[592,2304]{1,0:T(8,128)(2,1)S(1)} %add_convert_fusion.q_ref.k_ref.v_ref, bf16[592,2304]{1,0:T(8,128)(2,1)S(1)} %add_convert_fusion.q_ref.k_ref.v_ref, bf16[592,2304]{1,0:T(8,128)(2,1)S(1)} %add_convert_fusion.q_ref.k_ref.v_ref, ...), custom_call_target="tpu_custom_call" | custom-call | flops 2691563520 | bytes 3637248 | tf_op jit(solution)/shard_map/pallas_call | solution.py:161
  248.8 10.1 %collective-permute-done.36 = bf16[1,192,1152]{2,1,0:T(8,128)(2,1)S(1)} collective-permute-done((bf16[1,192,1152]{2,1,0:T(8,128)(2,1)S(1)}, bf16[1,192,1152]{2,1,0:T(8,128)(2,1)S(1)}, u32[]{:S(2)}, u32[]{:S(2)}) %collective-permute-start.36) | collective-permute-done | bytes 442400 | tf_op jit(solution)/shard_map/ppermute | solution.py:446
  267.5 10.2 %shard_map.277 = (bf16[3,592,384]{2,1,0:T(8,128)(2,1)}, f32[2,384]{1,0:T(2,128)S(1)}) custom-call(s32[1]{0:T(128)} %bitcast.63.place_ref, bf16[592,2304]{1,0:T(8,128)(2,1)S(1)} %add_convert_fusion.q_ref.k_ref.v_ref, bf16[592,2304]{1,0:T(8,128)(2,1)S(1)} %add_convert_fusion.q_ref.k_ref.v_ref, bf16[592,2304]{1,0:T(8,128)(2,1)S(1)} %add_convert_fusion.q_ref.k_ref.v_ref, ...), custom_call_target="tpu_custom_call" | custom-call | flops 2691563520 | bytes 3637248 | tf_op jit(solution)/shard_map/pallas_call | solution.py:161
  298.6 6.1 %shard_map.279 = f32[592,768]{1,0:T(8,128)S(1)} custom-call(s32[1]{0:T(128)} %bitcast.63.place_ref, bf16[3,592,384]{2,1,0:T(8,128)(2,1)S(1)} %copy-done.8, bf16[3,592,384]{2,1,0:T(8,128)(2,1)} %get-tuple-element.189.right_ref.near_ref, bf16[768,2304]{1,0:T(8,128)(2,1)S(1)} %bitcast.436), custom_call_target="tpu_custom_call" | custom-call | flops 2095054848 | bytes 10485760 | tf_op jit(solution)/shard_map/pallas_call | solution.py:650
  310.6 7.6 %collective-permute-done.46 = bf16[1,384,1152]{2,1,0:T(8,128)(2,1)S(1)} collective-permute-done((bf16[1,384,1152]{2,1,0:T(8,128)(2,1)}, bf16[1,384,1152]{2,1,0:T(8,128)(2,1)S(1)}, u32[]{:S(2)}, u32[]{:S(2)}) %collective-permute-start.46) | collective-permute-done | bytes 884768 | tf_op jit(solution)/shard_map/ppermute | solution.py:446
  346.8 10.4 %collective-permute-done.50 = bf16[1,384,640]{2,1,0:T(8,128)(2,1)S(1)} collective-permute-done((bf16[1,384,640]{2,1,0:T(8,128)(2,1)S(1)}, bf16[1,384,640]{2,1,0:T(8,128)(2,1)S(1)}, u32[]{:S(2)}, u32[]{:S(2)}) %collective-permute-start.50) | collective-permute-done | bytes 491552 | tf_op jit(solution)/shard_map/ppermute | solution.py:446
  367.2 11.6 %collective-permute-done.55 = bf16[4,48,1280]{2,1,0:T(8,128)(2,1)S(1)} collective-permute-done((bf16[4,48,1280]{2,1,0:T(8,128)(2,1)}, bf16[4,48,1280]{2,1,0:T(8,128)(2,1)S(1)}, u32[]{:S(2)}, u32[]{:S(2)}) %collective-permute-start.55) | collective-permute-done | bytes 491552 | tf_op jit(solution)/shard_map/ppermute | solution.py:446
  383.6 12.2 %collective-permute-done.56 = bf16[4,48,1280]{2,1,0:T(8,128)(2,1)} collective-permute-done((bf16[4,48,1280]{2,1,0:T(8,128)(2,1)}, bf16[4,48,1280]{2,1,0:T(8,128)(2,1)}, u32[]{:S(2)}, u32[]{:S(2)}) %collective-permute-start.56) | collective-permute-done | bytes 491552 | tf_op jit(solution)/shard_map/ppermute | solution.py:1247
  424.1 6.4 %collective-permute-done.64 = bf16[48,1664]{1,0:T(8,128)(2,1)S(1)} collective-permute-done((bf16[48,1664]{1,0:T(8,128)(2,1)S(1)}, bf16[48,1664]{1,0:T(8,128)(2,1)S(1)}, u32[]{:S(2)}, u32[]{:S(2)}) %collective-permute-start.64) | collective-permute-done | bytes 159776 | tf_op jit(solution)/shard_map/ppermute | solution.py:446
  434.7 5.9 %collective-permute-done.67 = bf16[48,1664]{1,0:T(8,128)(2,1)S(1)} collective-permute-done((bf16[48,1664]{1,0:T(8,128)(2,1)S(1)}, bf16[48,1664]{1,0:T(8,128)(2,1)S(1)}, u32[]{:S(2)}, u32[]{:S(2)}) %collective-permute-start.67) | collective-permute-done | bytes 159776 | tf_op jit(solution)/shard_map/ppermute | solution.py:446
  445.7 8.4 %collective-permute-done.69 = bf16[48,1664]{1,0:T(8,128)(2,1)S(1)} collective-permute-done((bf16[48,1664]{1,0:T(8,128)(2,1)S(1)}, bf16[48,1664]{1,0:T(8,128)(2,1)S(1)}, u32[]{:S(2)}, u32[]{:S(2)}) %collective-permute-start.69) | collective-permute-done | bytes 159776 | tf_op jit(solution)/shard_map/ppermute | solution.py:446
  454.9 37.6 %shard_map.282 = bf16[192,3072]{1,0:T(8,128)(2,1)S(1)} custom-call(s32[1]{0:T(128)} %bitcast.120.squares_ref, bf16[8,96,1536]{2,1,0:T(8,128)(2,1)S(1)} %pad_maximum_fusion.own_ref, bf16[8,96,1536]{2,1,0:T(8,128)(2,1)} %collective-permute-done.68.other_ref), custom_call_target="tpu_custom_call" | custom-call | flops 40768634880 | bytes 8388608 | tf_op jit(solution)/shard_map/pallas_call | solution.py:402
  504.1 10.5 %collective-permute-done.71 = bf16[48,3072]{1,0:T(8,128)(2,1)S(1)} collective-permute-done((bf16[48,3072]{1,0:T(8,128)(2,1)S(1)}, bf16[48,3072]{1,0:T(8,128)(2,1)S(1)}, u32[]{:S(2)}, u32[]{:S(2)}) %collective-permute-start.71) | collective-permute-done | bytes 294944 | tf_op jit(solution)/shard_map/ppermute | solution.py:446
  514.5 7.1 %collective-permute-done.72 = bf16[48,3072]{1,0:T(8,128)(2,1)S(1)} collective-permute-done((bf16[48,3072]{1,0:T(8,128)(2,1)S(1)}, bf16[48,3072]{1,0:T(8,128)(2,1)S(1)}, u32[]{:S(2)}, u32[]{:S(2)}) %collective-permute-start.72) | collective-permute-done | bytes 294944 | tf_op jit(solution)/shard_map/ppermute | solution.py:446
  (670 shorter events, 291.4 us)
Async XLA Ops:
  42.0 38.6 %collective-permute-start.9 = (bf16[592,768]{1,0:T(8,128)(2,1)}, bf16[592,768]{1,0:T(8,128)(2,1)}, u32[]{:S(2)}, u32[]{:S(2)}) collective-permute-start(bf16[592,768]{1,0:T(8,128)(2,1)} %pad.25.left_ref), channel_id=1, source_target_pairs={{0,2},{1,3},{2,0},{3,1},{4,6},{5,7},{6,4},{7,5},{8,10},{9,11},{10,... | collective-permute-start | bytes 2727944 | tf_op jit(solution)/shard_map/ppermute | solution.py:446
  76.3 26.4 %collective-permute-start.14 = (bf16[592,768]{1,0:T(8,128)(2,1)S(1)}, bf16[592,768]{1,0:T(8,128)(2,1)S(1)}, u32[]{:S(2)}, u32[]{:S(2)}) collective-permute-start(bf16[592,768]{1,0:T(8,128)(2,1)S(1)} %add_convert_fusion.3.left_ref), channel_id=1, source_target_pairs={{0,2},{1,3},{2,0},{3,1},{4,6},{5,7},{6,4},{7,5},{8,10},{9,11},{10,... | collective-permute-start | bytes 2727944 | tf_op jit(solution)/shard_map/ppermute | solution.py:446
  83.0 19.8 %collective-permute-start.17 = (bf16[2,48,1920]{2,1,0:T(8,128)(2,1)S(1)}, bf16[2,48,1920]{2,1,0:T(8,128)(2,1)S(1)}, u32[]{:S(2)}, u32[]{:S(2)}) collective-permute-start(bf16[2,48,1920]{2,1,0:T(8,128)(2,1)S(1)} %get-tuple-element.382), channel_id=1, source_target_pairs={{0,8},{1,9},{2,10},{3,11},{4,12},{5,13},{6,14},{7,15},{8,0},{9,1},... | collective-permute-start | bytes 1105928 | tf_op jit(solution)/shard_map/ppermute | solution.py:446
  88.0 18.5 %collective-permute-start.16 = (bf16[2,4,48,1024]{3,2,1,0:T(8,128)(2,1)S(1)}, bf16[2,4,48,1024]{3,2,1,0:T(8,128)(2,1)S(1)}, u32[]{:S(2)}, u32[]{:S(2)}) collective-permute-start(bf16[2,4,48,1024]{3,2,1,0:T(8,128)(2,1)S(1)} %pad_maximum_fusion.17), channel_id=1, source_target_pairs={{0,4},{1,5},{2,6},{3,7},{4,0},{5,1},{6,2},{7,3},{8,12},{9,13},{10,... | collective-permute-start | bytes 2359304 | tf_op jit(solution)/shard_map/ppermute | solution.py:446
  109.7 36.5 %collective-permute-start.23 = (bf16[592,768]{1,0:T(8,128)(2,1)}, bf16[592,768]{1,0:T(8,128)(2,1)}, u32[]{:S(2)}, u32[]{:S(2)}) collective-permute-start(bf16[592,768]{1,0:T(8,128)(2,1)} %get-tuple-element.138.left_ref), channel_id=1, source_target_pairs={{0,2},{1,3},{2,0},{3,1},{4,6},{5,7},{6,4},{7,5},{8,10},{9,11},{10,... | collective-permute-start | bytes 2727944 | tf_op jit(solution)/shard_map/ppermute | solution.py:446
  122.4 23.8 %collective-permute-start.26 = (bf16[2,4,48,1024]{3,2,1,0:T(8,128)(2,1)}, bf16[2,4,48,1024]{3,2,1,0:T(8,128)(2,1)}, u32[]{:S(2)}, u32[]{:S(2)}) collective-permute-start(bf16[2,4,48,1024]{3,2,1,0:T(8,128)(2,1)} %pad_maximum_fusion.18), channel_id=1, source_target_pairs={{0,4},{1,5},{2,6},{3,7},{4,0},{5,1},{6,2},{7,3},{8,12},{9,13},{10,... | collective-permute-start | bytes 2359304 | tf_op jit(solution)/shard_map/ppermute | solution.py:446
  123.8 22.4 %collective-permute-start.24 = (bf16[592,768]{1,0:T(8,128)(2,1)}, bf16[592,768]{1,0:T(8,128)(2,1)}, u32[]{:S(2)}, u32[]{:S(2)}) collective-permute-start(bf16[592,768]{1,0:T(8,128)(2,1)} %add_convert_fusion.2.normed_ref.left_ref), channel_id=1, source_target_pairs={{0,2},{1,3},{2,0},{3,1},{4,6},{5,7},{6,4},{7,5},{8,10},{9,11},{10,... | collective-permute-start | bytes 2727944 | tf_op jit(solution)/shard_map/ppermute | solution.py:446
  125.0 21.2 %collective-permute-start.25 = (bf16[2,4,48,896]{3,2,1,0:T(8,128)(2,1)}, bf16[2,4,48,896]{3,2,1,0:T(8,128)(2,1)S(1)}, u32[]{:S(2)}, u32[]{:S(2)}) collective-permute-start(bf16[2,4,48,896]{3,2,1,0:T(8,128)(2,1)} %pad_maximum_fusion.22), channel_id=1, source_target_pairs={{0,1},{1,0},{2,3},{3,2},{4,5},{5,4},{6,7},{7,6},{8,9},{9,8},{10,11... | collective-permute-start | bytes 2064392 | tf_op jit(solution)/shard_map/ppermute | solution.py:446
  155.5 24.2 %collective-permute-start.30 = (bf16[592,3072]{1,0:T(8,128)(2,1)}, bf16[592,3072]{1,0:T(8,128)(2,1)}, u32[]{:S(2)}, u32[]{:S(2)}) collective-permute-start(bf16[592,3072]{1,0:T(8,128)(2,1)} %copy-done), channel_id=1, source_target_pairs={{0,2},{1,3},{2,0},{3,1},{4,6},{5,7},{6,4},{7,5},{8,10},{9,11},{10,... | collective-permute-start | bytes 10911752 | tf_op jit(solution)/shard_map/ppermute | solution.py:446
  210.4 22.1 %collective-permute-start.33 = (bf16[1,384,1152]{2,1,0:T(8,128)(2,1)}, bf16[1,384,1152]{2,1,0:T(8,128)(2,1)S(1)}, u32[]{:S(2)}, u32[]{:S(2)}) collective-permute-start(bf16[1,384,1152]{2,1,0:T(8,128)(2,1)} %pad_maximum_fusion.14), channel_id=1, source_target_pairs={{0,1},{1,0},{2,3},{3,2},{4,5},{5,4},{6,7},{7,6},{8,9},{9,8},{10,11... | collective-permute-start | bytes 2654216 | tf_op jit(solution)/shard_map/ppermute | solution.py:446
  210.9 22.7 %collective-permute-start.37 = (bf16[2,192,768]{2,1,0:T(8,128)(2,1)}, bf16[2,192,768]{2,1,0:T(8,128)(2,1)S(1)}, u32[]{:S(2)}, u32[]{:S(2)}) collective-permute-start(bf16[2,192,768]{2,1,0:T(8,128)(2,1)} %bitcast.456), channel_id=1, source_target_pairs={{0,4},{1,5},{2,6},{3,7},{4,0},{5,1},{6,2},{7,3},{8,12},{9,13},{10,... | collective-permute-start | bytes 1769480 | tf_op jit(solution)/shard_map/ppermute | solution.py:446
  228.0 32.8 %collective-permute-start.41 = (bf16[2,192,1152]{2,1,0:T(8,128)(2,1)S(1)}, bf16[2,192,1152]{2,1,0:T(8,128)(2,1)S(1)}, u32[]{:S(2)}, u32[]{:S(2)}) collective-permute-start(bf16[2,192,1152]{2,1,0:T(8,128)(2,1)S(1)} %pad_maximum_fusion.15), channel_id=1, source_target_pairs={{0,4},{1,5},{2,6},{3,7},{4,0},{5,1},{6,2},{7,3},{8,12},{9,13},{10,... | collective-permute-start | bytes 2654216 | tf_op jit(solution)/shard_map/ppermute | solution.py:446
  235.5 23.5 %collective-permute-start.36 = (bf16[1,192,1152]{2,1,0:T(8,128)(2,1)S(1)}, bf16[1,192,1152]{2,1,0:T(8,128)(2,1)S(1)}, u32[]{:S(2)}, u32[]{:S(2)}) collective-permute-start(bf16[1,192,1152]{2,1,0:T(8,128)(2,1)S(1)} %pad_maximum_fusion.29), channel_id=1, source_target_pairs={{0,4},{1,5},{2,6},{3,7},{4,0},{5,1},{6,2},{7,3},{8,12},{9,13},{10,... | collective-permute-start | bytes 1327112 | tf_op jit(solution)/shard_map/ppermute | solution.py:446
  237.0 22.8 %collective-permute-start.39 = (bf16[1,384,768]{2,1,0:T(8,128)(2,1)S(1)}, bf16[1,384,768]{2,1,0:T(8,128)(2,1)S(1)}, u32[]{:S(2)}, u32[]{:S(2)}) collective-permute-start(bf16[1,384,768]{2,1,0:T(8,128)(2,1)S(1)} %bitcast.457), channel_id=1, source_target_pairs={{0,1},{1,0},{2,3},{3,2},{4,5},{5,4},{6,7},{7,6},{8,9},{9,8},{10,11... | collective-permute-start | bytes 1769480 | tf_op jit(solution)/shard_map/ppermute | solution.py:446
  277.9 68.9 %collective-permute-start.51 = (f32[48,1536]{1,0:T(8,128)}, f32[48,1536]{1,0:T(8,128)}, u32[]{:S(2)}, u32[]{:S(2)}) collective-permute-start(f32[48,1536]{1,0:T(8,128)} %get-tuple-element.317), channel_id=1, source_target_pairs={{0,16},{1,17},{2,18},{3,19},{4,20},{5,21},{6,22},{7,23},{8,24},{9,... | collective-permute-start | bytes 884744 | tf_op jit(solution)/shard_map/ppermute | solution.py:446
  278.7 81.9 %collective-permute-start.54 = (f32[48,1536]{1,0:T(8,128)}, f32[48,1536]{1,0:T(8,128)}, u32[]{:S(2)}, u32[]{:S(2)}) collective-permute-start(f32[48,1536]{1,0:T(8,128)} %get-tuple-element.316), channel_id=1, source_target_pairs={{0,24},{1,25},{2,26},{3,27},{4,28},{5,29},{6,30},{7,31},{8,16},{9,... | collective-permute-start | bytes 884744 | tf_op jit(solution)/shard_map/ppermute | solution.py:446
  287.1 17.7 %collective-permute-start.44 = (bf16[1,192,1152]{2,1,0:T(8,128)(2,1)}, bf16[1,192,1152]{2,1,0:T(8,128)(2,1)S(1)}, u32[]{:S(2)}, u32[]{:S(2)}) collective-permute-start(bf16[1,192,1152]{2,1,0:T(8,128)(2,1)} %pad_maximum_fusion.30), channel_id=1, source_target_pairs={{0,1},{1,0},{2,3},{3,2},{4,5},{5,4},{6,7},{7,6},{8,9},{9,8},{10,11... | collective-permute-start | bytes 1327112 | tf_op jit(solution)/shard_map/ppermute | solution.py:446
  291.5 26.8 %collective-permute-start.46 = (bf16[1,384,1152]{2,1,0:T(8,128)(2,1)}, bf16[1,384,1152]{2,1,0:T(8,128)(2,1)S(1)}, u32[]{:S(2)}, u32[]{:S(2)}) collective-permute-start(bf16[1,384,1152]{2,1,0:T(8,128)(2,1)} %bitcast.440), channel_id=1, source_target_pairs={{0,1},{1,0},{2,3},{3,2},{4,5},{5,4},{6,7},{7,6},{8,9},{9,8},{10,11... | collective-permute-start | bytes 2654216 | tf_op jit(solution)/shard_map/ppermute | solution.py:446
  307.5 22.5 %collective-permute-start.45 = (bf16[4,48,1536]{2,1,0:T(8,128)(2,1)}, bf16[4,48,1536]{2,1,0:T(8,128)(2,1)}, u32[]{:S(2)}, u32[]{:S(2)}) collective-permute-start(bf16[4,48,1536]{2,1,0:T(8,128)(2,1)} %select_convert_fusion.1), channel_id=1, source_target_pairs={{0,8},{1,9},{2,10},{3,11},{4,12},{5,13},{6,14},{7,15},{8,0},{9,1},... | collective-permute-start | bytes 1769480 | tf_op jit(solution)/shard_map/ppermute | solution.py:446
  320.4 25.2 %collective-permute-start.52 = (bf16[1,192,1152]{2,1,0:T(8,128)(2,1)}, bf16[1,192,1152]{2,1,0:T(8,128)(2,1)}, u32[]{:S(2)}, u32[]{:S(2)}) collective-permute-start(bf16[1,192,1152]{2,1,0:T(8,128)(2,1)} %slice.730), channel_id=1, source_target_pairs={{0,4},{1,5},{2,6},{3,7},{4,0},{5,1},{6,2},{7,3},{8,12},{9,13},{10,... | collective-permute-start | bytes 1327112 | tf_op jit(solution)/shard_map/ppermute | solution.py:446
  332.6 26.4 %collective-permute-start.48 = (bf16[4,48,1536]{2,1,0:T(8,128)(2,1)}, bf16[4,48,1536]{2,1,0:T(8,128)(2,1)}, u32[]{:S(2)}, u32[]{:S(2)}) collective-permute-start(bf16[4,48,1536]{2,1,0:T(8,128)(2,1)} %fusion.176), channel_id=1, source_target_pairs={{8,24},{9,25},{10,26},{11,27},{12,28},{13,29},{14,30},{15,31},{16,... | collective-permute-start | bytes 1769480 | tf_op jit(solution)/shard_map/ppermute | solution.py:1211
  454.3 42.0 %collective-permute-start.73 = (bf16[4,48,1664]{2,1,0:T(8,128)(2,1)S(1)}, bf16[4,48,1664]{2,1,0:T(8,128)(2,1)S(1)}, u32[]{:S(2)}, u32[]{:S(2)}) collective-permute-start(bf16[4,48,1664]{2,1,0:T(8,128)(2,1)S(1)} %get-tuple-element.356), channel_id=1, source_target_pairs={{0,1},{1,0},{2,3},{3,2},{4,5},{5,4},{6,7},{7,6},{8,9},{9,8},{10,11... | collective-permute-start | bytes 1916936 | tf_op jit(solution)/shard_map/ppermute | solution.py:446
  492.7 21.8 %collective-permute-start.71 = (bf16[48,3072]{1,0:T(8,128)(2,1)S(1)}, bf16[48,3072]{1,0:T(8,128)(2,1)S(1)}, u32[]{:S(2)}, u32[]{:S(2)}) collective-permute-start(bf16[48,3072]{1,0:T(8,128)(2,1)S(1)} %get-tuple-element.306), channel_id=1, source_target_pairs={{0,16},{1,17},{2,18},{3,19},{4,20},{5,21},{6,22},{7,23},{8,24},{9,... | collective-permute-start | bytes 884744 | tf_op jit(solution)/shard_map/ppermute | solution.py:446
  494.4 27.2 %collective-permute-start.72 = (bf16[48,3072]{1,0:T(8,128)(2,1)S(1)}, bf16[48,3072]{1,0:T(8,128)(2,1)S(1)}, u32[]{:S(2)}, u32[]{:S(2)}) collective-permute-start(bf16[48,3072]{1,0:T(8,128)(2,1)S(1)} %get-tuple-element.305), channel_id=1, source_target_pairs={{0,24},{1,25},{2,26},{3,27},{4,28},{5,29},{6,30},{7,31},{8,16},{9,... | collective-permute-start | bytes 884744 | tf_op jit(solution)/shard_map/ppermute | solution.py:446
  (180 other events, 1190.3 us)

commit v2 on v1

--- a/solution.py
+++ b/solution.py
@@ -147,7 +147,7 @@
         cost_estimate=cost(
             flops=8 * TOKENS * TOKENS * D, bytes_accessed=8 * TOKENS * D, transcendentals=0
         ),
-        compiler_params=pltpu.CompilerParams(vmem_limit_bytes=24 * MIB),
+        compiler_params=pltpu.CompilerParams(vmem_limit_bytes=18 * MIB),
     )(mixed, mixed, mixed, keep)
 
 
@@ -185,7 +185,7 @@
             bytes_accessed=16 * TOKENS * pairs * lanes,
             transcendentals=0,
         ),
-        compiler_params=pltpu.CompilerParams(vmem_limit_bytes=28 * MIB),
+        compiler_params=pltpu.CompilerParams(vmem_limit_bytes=20 * MIB),
     )(part.reshape(1).astype(jnp.int32), mixed, mixed, mixed, grad, logsum, keep)
 
 
@@ -205,8 +205,7 @@
 
 def gelu_parts(values):
     size = 1.0 + 0.23164189 * jnp.abs(values)
-    inner = pl.reciprocal(size, approx=True)
-    inner = inner * (2.0 - size * inner)
+    inner = 1.0 / size
     poly = jnp.full_like(inner, 0.5 * 1.061405429)
     for coeff in (-1.453152027, 1.421413741, -0.284496736, 0.254829592):
         poly = poly * inner + 0.5 * coeff
@@ -416,7 +415,7 @@
         cost_estimate=cost(
             flops=10 * D * D * (2 * FF + D), bytes_accessed=8 * MIB, transcendentals=0
         ),
-        compiler_params=pltpu.CompilerParams(vmem_limit_bytes=44 * MIB),
+        compiler_params=pltpu.CompilerParams(vmem_limit_bytes=36 * MIB),
     )(squares, own, other)
 
 
@@ -792,6 +791,10 @@
     def far(self, hold):
         self.first_far, self.last_far = together(self.first_far, self.last_far, *hold)[:2]
 
+    def swap_near(self):
+        self.first_core = self.wires.swap(self.first, self.wires.core_bit)
+        self.last_core = self.wires.swap(self.last, self.wires.core_bit)
+
     def send_far(self):
         wires = self.wires
         self.first_far = wires.swap(self.first, wires.dp_bits[0])
@@ -800,21 +803,27 @@
     def finish(self):
         wires, widths, split = self.wires, self.widths, self.split
         block = self.first.shape[2]
+        core_bit = wires.core_bit
         arrays = [
-            jnp.concatenate([self.first, self.first_far]), jnp.concatenate([self.last, self.last_far])
+            self.first,
+            self.first_far,
+            self.last,
+            self.last_far,
+            self.first_core,
+            wires.swap(self.first_far, core_bit),
+            self.last_core,
+            wires.swap(self.last_far, core_bit),
         ]
-        arrays += [wires.swap(item, wires.core_bit) for item in arrays]
         pieces = []
         for far_core in range(2):
             for far in range(2):
                 for index in range(2):
                     start = 0
-                    place = 2 * far + index
                     for matrix, width in enumerate(widths[:-1] + [split]):
-                        source = (2 * far_core, place)
+                        source = (4 * far_core + far, index)
                         pieces.append((source, index, far_core, far, start, matrix, 0, width))
                         start += width
-                    source = (2 * far_core + 1, place)
+                    source = (4 * far_core + 2 + far, index)
                     width = widths[-1] - split
                     pieces.append((source, far, far_core, index, 0, len(widths) - 1, split, width))
         place = jnp.stack(
@@ -831,7 +840,7 @@
             cost_estimate=cost(
                 flops=0, bytes_accessed=4 * D * 2 * sum(widths), transcendentals=0
             ),
-            compiler_params=pltpu.CompilerParams(vmem_limit_bytes=40 * MIB),
+            compiler_params=pltpu.CompilerParams(vmem_limit_bytes=16 * MIB),
         )(place.astype(jnp.int32), *arrays)
         return [whole.reshape(D, whole.shape[-1]) for whole in wholes]
 
@@ -867,6 +876,49 @@
     chosen_float = chosen.astype(float32)[:, None]
     mask_local = jnp.sum(chosen_float)
 
+    down_moment, down_master = muon_down.T, w_down.T
+    stride = -(-D // dp_size // 128) * 128
+    share = max(FF // dp_size, 3 * stride)
+    def sub_columns(parts):
+        return side_by_side([dp_columns(wires, item) for item in parts], stride, share)
+
+    def thirds(values):
+        return [values[:, index * D : (index + 1) * D] for index in range(3)]
+
+    moment_parts = jnp.stack(
+        [
+            padded_to(dp_columns(wires, down_moment), share),
+            sub_columns(thirds(muon_qkv)),
+            sub_columns([muon_square[index] for index in range(3)]),
+            padded_to(dp_columns(wires, muon_up), share),
+        ]
+    )
+    def for_groups(blocks):
+        return [
+            lax.dynamic_index_in_dim(blocks, wires.group ^ step, 0, keepdims=False)
+            for step in range(4)
+        ]
+
+    def send_groups(blocks):
+        blocks = for_groups(blocks) if not isinstance(blocks, list) else blocks
+        return blocks[:1] + [
+            wires.swap_mask(blocks[step], step << wires.near_bit) for step in (1, 2, 3)
+        ]
+
+    def by_group(got):
+        got = jnp.stack(got)
+        return jnp.stack(
+            [
+                lax.dynamic_index_in_dim(got, group ^ wires.group, 0, keepdims=False)
+                for group in range(4)
+            ]
+        )
+
+    def across_groups(blocks):
+        return by_group(send_groups(blocks))
+
+    moment_blocks = for_groups(moment_parts)
+
     half = SMALL_PAD // 2
     used = -(-SMALL_ROWS // 2)
     small_low = small.astype(bfloat).T
@@ -910,7 +962,8 @@
         early.near()
         early.send_far()
         middle_own = doubled(wires, middle_own, far_bit)
-        early.far((middle_own,))
+        early.swap_near()
+        early.far((middle_own, early.first_core, early.last_core, *moment_blocks))
         embed_weight, small_whole, qkv_weight = early.finish()
         counts = small_whole.reshape(D, 2, half)[:, :, used : used + 2].astype(float32)
         mask_count = (256.0 * jnp.sum(counts[:, :, 0]) + jnp.sum(counts[:, :, 1])) / block
@@ -927,47 +980,7 @@
         [small_whole[:, :used], small_whole[:, half : half + SMALL_ROWS - used]], axis=1
     ).T.astype(float32)
 
-    down_moment, down_master = muon_down.T, w_down.T
-    stride = -(-D // dp_size // 128) * 128
-    share = max(FF // dp_size, 3 * stride)
-    def sub_columns(parts):
-        return side_by_side([dp_columns(wires, item) for item in parts], stride, share)
-
-    def thirds(values):
-        return [values[:, index * D : (index + 1) * D] for index in range(3)]
-
-    moment_parts = jnp.stack(
-        [
-            padded_to(dp_columns(wires, down_moment), share),
-            sub_columns(thirds(muon_qkv)),
-            sub_columns([muon_square[index] for index in range(3)]),
-            padded_to(dp_columns(wires, muon_up), share),
-        ]
-    )
-    if staged:
-        moment_parts = after(moment_parts, embed_weight)
-
-    def send_groups(blocks):
-        mine = wires.group
-        got = [lax.dynamic_index_in_dim(blocks, mine, 0, keepdims=False)]
-        for step in (1, 2, 3):
-            sent = lax.dynamic_index_in_dim(blocks, mine ^ step, 0, keepdims=False)
-            got.append(wires.swap_mask(sent, step << wires.near_bit))
-        return got
-
-    def by_group(got):
-        got = jnp.stack(got)
-        return jnp.stack(
-            [
-                lax.dynamic_index_in_dim(got, group ^ wires.group, 0, keepdims=False)
-                for group in range(4)
-            ]
-        )
-
-    def across_groups(blocks):
-        return by_group(send_groups(blocks))
-
-    moments_got = send_groups(moment_parts)
+    moments_got = send_groups(moment_blocks)
 
     long_table, short_table = interp_tables()
     table = jnp.where(long_image, long_table, short_table)
@@ -995,6 +1008,7 @@
     if staged:
         late_own = doubled(wires, late_own, far_bit, (mixed,))
         middle.near((mixed,))
+        middle.swap_near()
         mixed = after(mixed, middle.first, middle.last, late_own)
         middle.send_far()
     context_low, logsum = attend_forward(mixed, keep)
@@ -1011,7 +1025,8 @@
     up_bias = params_small[14 : 14 + UP_ROWS].reshape(-1)
     if staged:
         late.near((normed_second,))
-        normed_second = after(normed_second, late.first, late.last)
+        late.swap_near()
+        normed_second = after(normed_second, late.first, late.last, late.first_core, late.last_core)
         late.send_far()
     second_both = (normed_second, wires.swap(normed_second, wires.core_bit))
     activ_low, slope = up_forward(normed_second, up_weight, up_bias[None])
@@ -1289,14 +1304,14 @@
         [upper.reshape(-1, half_rows, share), lower.reshape(-1, half_rows, share)]
     )
     other_pieces = other(own_pieces)
-    other_pieces, grads_got[3] = together(other_pieces, grads_got[3])
-    grad_rows = by_group(grads_got)
-    grad_all = gather_relative(wires, grad_rows, dps).reshape((dp_size,) + grad_rows.shape)
-    own_pieces = after(own_pieces, grad_rows)
     squares_flag = (wires.group == 2).astype(jnp.int32).reshape(1)
     ortho = orthogonalize(
         squares_flag, own_pieces, other_pieces, 1 << len(rows), dp_size, stride, 4 * block
     )
+
+    ortho, grads_got[3] = together(ortho, grads_got[3])
+    grad_rows = by_group(grads_got)
+    grad_all = gather_relative(wires, grad_rows, dps).reshape((dp_size,) + grad_rows.shape)
 
     updates_got = send_groups(ortho.reshape(4, block, ortho.shape[1]))
 

time: 538 us -> 535 us (level)
  local copies, waits for them, and re-layouts: 54.4 us -> 71.4 us
  waiting for transfers between devices: 158 us -> 143 us
  other arithmetic: 71.2 us -> 60 us
  starting transfers between devices: 65.6 us -> 76.5 us
    ppermute x72 -> x78, waiting for transfers between devices: 145 us -> 130 us  [swap_mask(): lax.ppermute(values, BOTH, [(i, i ^ mask) for i in range(self.count)])]
    unnamed x264 -> x294, local copies, waits for them, and re-layouts: 29.7 us -> 44.5 us
    ppermute x72 -> x78, starting transfers between devices: 60.2 us -> 71 us  [swap_mask(): lax.ppermute(values, BOTH, [(i, i ^ mask) for i in range(self.count)])]
    concatenate x6 -> x0, other arithmetic: 7.45 us -> none  [the longest x3 4.75 us: finish(): jnp.concatenate([self.last, self.last_far])]
  transfers between devices with their start and end apart: 74 -> 80, of which waited for: 34 -> 33; matrix products, arithmetic and copies ran while one was open for 18% -> 16% of each run, Pallas kernels for 21% -> 21%
where the time goes in v2:
time: 535 us; the launch traced here: 525 us
  waiting for transfers between devices  143 us (27%)
  Pallas kernels  139 us (26%)
  starting transfers between devices  76.5 us (14%)
  local copies, waits for them, and re-layouts  71.4 us (13%)
  other arithmetic  60 us (11%)
  matrix products  24.4 us (5%)
  between operations  11.4 us (2%)
    ppermute x78, waiting for transfers between devices, swap_mask(): lax.ppermute(values, BOTH, [(i, i ^ mask) for i in range(self.count)])  130 us
    ppermute x78, starting transfers between devices, swap_mask(): lax.ppermute(values, BOTH, [(i, i ^ mask) for i in range(self.count)])  71 us
    unnamed x294, local copies, waits for them, and re-layouts  44.5 us
    pallas_call x1, Pallas kernels, orthogonalize(): pl.pallas_call(partial(ortho_kernel, places=places, shares=shares, stride...  37.6 us
    pallas_call x7, Pallas kernels, pair_grad(): pl.pallas_call(partial(pair_kernel, by_rows=by_rows, halves=halves), grid...  33.9 us
    pallas_call x2, Pallas kernels, attend_backward(): pl.pallas_call(attend_backward_kernel, grid_spec=pltpu.PrefetchScalarGrid...  19.4 us
    dot_general x7, matrix products, dot_nt(): lax.dot_general(left, right, (((1,), (1,)), ((), ())), preferred_element_...  14.2 us
    pallas_call x1, Pallas kernels, attend_forward(): pl.pallas_call(attend_forward_kernel, grid=(PAIRS,), in_specs=[head_block...  12.5 us
  transfers between devices with their start and end apart: 80, of which 33 were waited for; matrix products, arithmetic and copies ran while one was open for 16% of the time, Pallas kernels for 21%

profile of v2, /device:TPU:20, one launch (start us, length us, event | category | flops | bytes accessed | tf_op | source)
XLA Modules:
  0.0 525.0 jit_solution(2768610642051972528)
XLA Ops:
  18.1 4.6 collective-permute-start.1
  24.8 5.6 %collective-permute-done.1 = bf16[2,48,1664]{2,1,0:T(8,128)(2,1)S(1)} collective-permute-done((bf16[2,48,1664]{2,1,0:T(8,128)(2,1)S(1)}, bf16[2,48,1664]{2,1,0:T(8,128)(2,1)S(1)}, u32[]{:S(2)}, u32[]{:S(2)}) %collective-permute-start.1) | collective-permute-done | bytes 319520 | tf_op jit(solution)/shard_map/ppermute | solution.py:445
  33.0 6.2 %collective-permute-done.2 = bf16[4,48,768]{2,1,0:T(8,128)(2,1)S(1)} collective-permute-done((bf16[4,48,768]{2,1,0:T(8,128)(2,1)S(1)}, bf16[4,48,768]{2,1,0:T(8,128)(2,1)S(1)}, u32[]{:S(2)}, u32[]{:S(2)}) %collective-permute-start.2) | collective-permute-done | bytes 294944 | tf_op jit(solution)/shard_map/ppermute | solution.py:445
  44.4 7.8 %collective-permute-done.6 = bf16[48,1920]{1,0:T(8,128)(2,1)S(1)} collective-permute-done((bf16[48,1920]{1,0:T(8,128)(2,1)S(1)}, bf16[48,1920]{1,0:T(8,128)(2,1)S(1)}, u32[]{:S(2)}, u32[]{:S(2)}) %collective-permute-start.6) | collective-permute-done | bytes 184352 | tf_op jit(solution)/shard_map/ppermute | solution.py:445
  54.0 4.7 collective-permute-done.5.refs_3_
  91.4 12.5 %shard_map.264 = (bf16[592,768]{1,0:T(8,128)(2,1)S(1)}, f32[12,1,592]{2,1,0:T(1,128)S(1)}) custom-call(bf16[592,2304]{1,0:T(8,128)(2,1)S(1)} %add_convert_fusion.q_ref.k_ref.v_ref, bf16[592,2304]{1,0:T(8,128)(2,1)S(1)} %add_convert_fusion.q_ref.k_ref.v_ref, bf16[592,2304]{1,0:T(8,128)(2,1)S(1)} %add_convert_fusion.q_ref.k_ref.v_ref, ...), custom_call_target="tpu_custom_call" | custom-call | flops 2153250816 | bytes 3637248 | tf_op jit(solution)/shard_map/pallas_call | solution.py:138
  130.2 9.3 %shard_map.266 = (bf16[592,3072]{1,0:T(8,128)(2,1)S(1)}, f32[592,3072]{1,0:T(8,128)S(1)}) custom-call(bf16[592,768]{1,0:T(8,128)(2,1)S(1)} %add_convert_fusion.2.normed_ref.left_ref, bf16[768,3072]{1,0:T(8,128)(2,1)S(1)} %bitcast.447, f32[1,3072]{1,0:T(1,128)S(1)} %bitcast.446), custom_call_target="tpu_custom_call" | custom-call | flops 2793406464 | bytes 20971520 | tf_op jit(solution)/shard_map/pallas_call | solution.py:233
  174.9 4.6 shard_map.269
  180.3 5.6 %shard_map.268 = (f32[1,1,384,768]{3,2,1,0:T(8,128)S(1)}, bf16[1,1,384,768]{3,2,1,0:T(8,128)(2,1)S(1)}) custom-call(s32[1]{0:T(128)} %bitcast.65.place_ref, bf16[384,768]{1,0:T(8,128)(2,1)S(1)} %fusion.8.select_ref, bf16[592,768]{1,0:T(8,128)(2,1)} %convert_element_type.408.left_ref.branch_ref, bf16[592,768]{1,0:T(8,128)(2,1)} %collective-permute-done.35.left_other_ref, ...), custom_call_target="tpu_custom_call" | custom-call | flops 1396703232 | bytes 4718592 | tf_op jit(solution)/shard_map/pallas_call | solution.py:579
  188.0 5.5 %shard_map.270 = (f32[2,1,192,768]{3,2,1,0:T(8,128)S(1)}, bf16[2,1,192,768]{3,2,1,0:T(8,128)(2,1)S(1)}) custom-call(s32[1]{0:T(128)} %bitcast.65.place_ref, bf16[384,768]{1,0:T(8,128)(2,1)S(1)} %fusion.8.select_ref, bf16[592,768]{1,0:T(8,128)(2,1)} %convert_element_type.408.left_ref.branch_ref, bf16[592,768]{1,0:T(8,128)(2,1)} %collective-permute-done.35.left_other_ref, ...), custom_call_target="tpu_custom_call" | custom-call | flops 1396703232 | bytes 4718592 | tf_op jit(solution)/shard_map/pallas_call | solution.py:579
  195.4 6.5 %shard_map.271 = (bf16[592,3072]{1,0:T(8,128)(2,1)}, f32[1,3072]{1,0:T(1,128)S(1)}) custom-call(bf16[592,768]{1,0:T(8,128)(2,1)} %convert_element_type.408.left_ref.branch_ref, bf16[768,3072]{1,0:T(8,128)(2,1)S(1)} %bitcast.432, f32[592,3072]{1,0:T(8,128)S(1)} %bitcast.428), custom_call_target="tpu_custom_call" | custom-call | flops 2793406464 | bytes 20971520 | tf_op jit(solution)/shard_map/pallas_call | solution.py:261
  202.0 6.2 %multiply_reduce_fusion.1 = (f32[768]{0:T(1024)}, f32[592]{0:T(1024)S(1)}, f32[592]{0:T(1024)S(1)}, f32[768]{0:T(1024)S(1)}, f32[592,768]{1,0:T(8,128)S(1)}) fusion(f32[592,768]{1,0:T(8,128)S(1)} %copy-done.64, f32[592]{0:T(1024)S(1)} %copy-done.130, f32[592]{0:T(1024)S(1)} %copy-done.120, f32[768]{0:T(1024)S(1)} %copy-done.128, ...), kind=kOutput, calls=%fused_computation.5 | convolution fusion | flops 2797495808 | bytes 12011776 | tf_op jit(solution)/shard_map/dot_general | solution.py:74
  216.9 4.9 shard_map.272
  221.9 4.9 shard_map.273
  239.4 9.2 %shard_map.275 = (bf16[3,592,384]{2,1,0:T(8,128)(2,1)S(1)}, f32[2,384]{1,0:T(2,128)S(1)}) custom-call(s32[1]{0:T(128)} %bitcast.77.place_ref, bf16[592,2304]{1,0:T(8,128)(2,1)S(1)} %add_convert_fusion.q_ref.k_ref.v_ref, bf16[592,2304]{1,0:T(8,128)(2,1)S(1)} %add_convert_fusion.q_ref.k_ref.v_ref, bf16[592,2304]{1,0:T(8,128)(2,1)S(1)} %add_convert_fusion.q_ref.k_ref.v_ref, ...), custom_call_target="tpu_custom_call" | custom-call | flops 2691563520 | bytes 3637248 | tf_op jit(solution)/shard_map/pallas_call | solution.py:161
  249.6 12.0 %collective-permute-done.42 = bf16[1,192,1152]{2,1,0:T(8,128)(2,1)S(1)} collective-permute-done((bf16[1,192,1152]{2,1,0:T(8,128)(2,1)S(1)}, bf16[1,192,1152]{2,1,0:T(8,128)(2,1)S(1)}, u32[]{:S(2)}, u32[]{:S(2)}) %collective-permute-start.42) | collective-permute-done | bytes 442400 | tf_op jit(solution)/shard_map/ppermute | solution.py:445
  270.2 10.2 %shard_map.277 = (bf16[3,592,384]{2,1,0:T(8,128)(2,1)}, f32[2,384]{1,0:T(2,128)S(1)}) custom-call(s32[1]{0:T(128)} %bitcast.65.place_ref, bf16[592,2304]{1,0:T(8,128)(2,1)S(1)} %add_convert_fusion.q_ref.k_ref.v_ref, bf16[592,2304]{1,0:T(8,128)(2,1)S(1)} %add_convert_fusion.q_ref.k_ref.v_ref, bf16[592,2304]{1,0:T(8,128)(2,1)S(1)} %add_convert_fusion.q_ref.k_ref.v_ref, ...), custom_call_target="tpu_custom_call" | custom-call | flops 2691563520 | bytes 3637248 | tf_op jit(solution)/shard_map/pallas_call | solution.py:161
  302.3 6.1 %shard_map.279 = f32[592,768]{1,0:T(8,128)S(1)} custom-call(s32[1]{0:T(128)} %bitcast.65.place_ref, bf16[3,592,384]{2,1,0:T(8,128)(2,1)S(1)} %copy-done.10, bf16[3,592,384]{2,1,0:T(8,128)(2,1)} %get-tuple-element.186.right_ref.near_ref, bf16[768,2304]{1,0:T(8,128)(2,1)S(1)} %bitcast.436), custom_call_target="tpu_custom_call" | custom-call | flops 2095054848 | bytes 10485760 | tf_op jit(solution)/shard_map/pallas_call | solution.py:649
  348.9 10.7 %collective-permute-done.56 = bf16[1,384,640]{2,1,0:T(8,128)(2,1)S(1)} collective-permute-done((bf16[1,384,640]{2,1,0:T(8,128)(2,1)S(1)}, bf16[1,384,640]{2,1,0:T(8,128)(2,1)S(1)}, u32[]{:S(2)}, u32[]{:S(2)}) %collective-permute-start.56) | collective-permute-done | bytes 491552 | tf_op jit(solution)/shard_map/ppermute | solution.py:445
  369.9 11.2 %collective-permute-done.61 = bf16[4,48,1280]{2,1,0:T(8,128)(2,1)S(1)} collective-permute-done((bf16[4,48,1280]{2,1,0:T(8,128)(2,1)}, bf16[4,48,1280]{2,1,0:T(8,128)(2,1)S(1)}, u32[]{:S(2)}, u32[]{:S(2)}) %collective-permute-start.61) | collective-permute-done | bytes 491552 | tf_op jit(solution)/shard_map/ppermute | solution.py:445
  385.9 12.2 %collective-permute-done.62 = bf16[4,48,1280]{2,1,0:T(8,128)(2,1)} collective-permute-done((bf16[4,48,1280]{2,1,0:T(8,128)(2,1)}, bf16[4,48,1280]{2,1,0:T(8,128)(2,1)}, u32[]{:S(2)}, u32[]{:S(2)}) %collective-permute-start.62) | collective-permute-done | bytes 491552 | tf_op jit(solution)/shard_map/ppermute | solution.py:1262
  438.3 4.6 collective-permute-done.73
  450.3 37.6 %shard_map.282 = bf16[192,3072]{1,0:T(8,128)(2,1)S(1)} custom-call(s32[1]{0:T(128)} %bitcast.120.squares_ref, bf16[8,96,1536]{2,1,0:T(8,128)(2,1)S(1)} %pad_maximum_fusion.own_ref, bf16[8,96,1536]{2,1,0:T(8,128)(2,1)} %collective-permute-done.74.other_ref), custom_call_target="tpu_custom_call" | custom-call | flops 40768634880 | bytes 8388608 | tf_op jit(solution)/shard_map/pallas_call | solution.py:401
  493.5 14.0 %collective-permute-done.79 = bf16[4,48,1664]{2,1,0:T(8,128)(2,1)S(1)} collective-permute-done((bf16[4,48,1664]{2,1,0:T(8,128)(2,1)S(1)}, bf16[4,48,1664]{2,1,0:T(8,128)(2,1)S(1)}, u32[]{:S(2)}, u32[]{:S(2)}) %collective-permute-start.79) | collective-permute-done | bytes 639008 | tf_op jit(solution)/shard_map/ppermute | solution.py:445
  (706 shorter events, 297.1 us)
Async XLA Ops:
  52.2 28.5 %collective-permute-start.11 = (bf16[592,768]{1,0:T(8,128)(2,1)}, bf16[592,768]{1,0:T(8,128)(2,1)}, u32[]{:S(2)}, u32[]{:S(2)}) collective-permute-start(bf16[592,768]{1,0:T(8,128)(2,1)} %pad.27.left_ref), channel_id=1, source_target_pairs={{0,2},{1,3},{2,0},{3,1},{4,6},{5,7},{6,4},{7,5},{8,10},{9,11},{10,... | collective-permute-start | bytes 2727944 | tf_op jit(solution)/shard_map/ppermute | solution.py:445
  76.4 27.6 %collective-permute-start.16 = (bf16[592,768]{1,0:T(8,128)(2,1)S(1)}, bf16[592,768]{1,0:T(8,128)(2,1)S(1)}, u32[]{:S(2)}, u32[]{:S(2)}) collective-permute-start(bf16[592,768]{1,0:T(8,128)(2,1)S(1)} %add_convert_fusion.3.left_ref), channel_id=1, source_target_pairs={{0,2},{1,3},{2,0},{3,1},{4,6},{5,7},{6,4},{7,5},{8,10},{9,11},{10,... | collective-permute-start | bytes 2727944 | tf_op jit(solution)/shard_map/ppermute | solution.py:445
  83.6 20.4 %collective-permute-start.19 = (bf16[2,48,1920]{2,1,0:T(8,128)(2,1)S(1)}, bf16[2,48,1920]{2,1,0:T(8,128)(2,1)S(1)}, u32[]{:S(2)}, u32[]{:S(2)}) collective-permute-start(bf16[2,48,1920]{2,1,0:T(8,128)(2,1)S(1)} %get-tuple-element.378), channel_id=1, source_target_pairs={{0,8},{1,9},{2,10},{3,11},{4,12},{5,13},{6,14},{7,15},{8,0},{9,1},... | collective-permute-start | bytes 1105928 | tf_op jit(solution)/shard_map/ppermute | solution.py:445
  88.0 19.0 %collective-permute-start.18 = (bf16[2,4,48,1024]{3,2,1,0:T(8,128)(2,1)S(1)}, bf16[2,4,48,1024]{3,2,1,0:T(8,128)(2,1)S(1)}, u32[]{:S(2)}, u32[]{:S(2)}) collective-permute-start(bf16[2,4,48,1024]{3,2,1,0:T(8,128)(2,1)S(1)} %pad_maximum_fusion.11.refs_2_), channel_id=1, source_target_pairs={{0,4},{1,5},{2,6},{3,7},{4,0},{5,1},{6,2},{7,3},{8,12},{9,13},{10,... | collective-permute-start | bytes 2359304 | tf_op jit(solution)/shard_map/ppermute | solution.py:445
  91.3 20.5 %collective-permute-start.22 = (bf16[2,4,48,1024]{3,2,1,0:T(8,128)(2,1)S(1)}, bf16[2,4,48,1024]{3,2,1,0:T(8,128)(2,1)S(1)}, u32[]{:S(2)}, u32[]{:S(2)}) collective-permute-start(bf16[2,4,48,1024]{3,2,1,0:T(8,128)(2,1)S(1)} %pad_maximum_fusion.11.refs_2_), channel_id=1, source_target_pairs={{0,2},{1,3},{2,0},{3,1},{4,6},{5,7},{6,4},{7,5},{8,10},{9,11},{10,... | collective-permute-start | bytes 2359304 | tf_op jit(solution)/shard_map/ppermute | solution.py:445
  122.3 22.1 %collective-permute-start.29 = (bf16[592,768]{1,0:T(8,128)(2,1)S(1)}, bf16[592,768]{1,0:T(8,128)(2,1)S(1)}, u32[]{:S(2)}, u32[]{:S(2)}) collective-permute-start(bf16[592,768]{1,0:T(8,128)(2,1)S(1)} %get-tuple-element.136.left_ref), channel_id=1, source_target_pairs={{0,2},{1,3},{2,0},{3,1},{4,6},{5,7},{6,4},{7,5},{8,10},{9,11},{10,... | collective-permute-start | bytes 2727944 | tf_op jit(solution)/shard_map/ppermute | solution.py:445
  126.8 19.9 %collective-permute-start.32 = (bf16[2,4,48,1024]{3,2,1,0:T(8,128)(2,1)S(1)}, bf16[2,4,48,1024]{3,2,1,0:T(8,128)(2,1)}, u32[]{:S(2)}, u32[]{:S(2)}) collective-permute-start(bf16[2,4,48,1024]{3,2,1,0:T(8,128)(2,1)S(1)} %pad_maximum_fusion.12.refs_2_), channel_id=1, source_target_pairs={{0,4},{1,5},{2,6},{3,7},{4,0},{5,1},{6,2},{7,3},{8,12},{9,13},{10,... | collective-permute-start | bytes 2359304 | tf_op jit(solution)/shard_map/ppermute | solution.py:445
  154.1 26.3 %collective-permute-start.36 = (bf16[592,3072]{1,0:T(8,128)(2,1)}, bf16[592,3072]{1,0:T(8,128)(2,1)}, u32[]{:S(2)}, u32[]{:S(2)}) collective-permute-start(bf16[592,3072]{1,0:T(8,128)(2,1)} %copy-done), channel_id=1, source_target_pairs={{0,2},{1,3},{2,0},{3,1},{4,6},{5,7},{6,4},{7,5},{8,10},{9,11},{10,... | collective-permute-start | bytes 10911752 | tf_op jit(solution)/shard_map/ppermute | solution.py:445
  211.5 22.1 %collective-permute-start.39 = (bf16[1,384,1152]{2,1,0:T(8,128)(2,1)}, bf16[1,384,1152]{2,1,0:T(8,128)(2,1)S(1)}, u32[]{:S(2)}, u32[]{:S(2)}) collective-permute-start(bf16[1,384,1152]{2,1,0:T(8,128)(2,1)} %pad_maximum_fusion.8), channel_id=1, source_target_pairs={{0,1},{1,0},{2,3},{3,2},{4,5},{5,4},{6,7},{7,6},{8,9},{9,8},{10,11... | collective-permute-start | bytes 2654216 | tf_op jit(solution)/shard_map/ppermute | solution.py:445
  213.0 22.2 %collective-permute-start.43 = (bf16[2,192,768]{2,1,0:T(8,128)(2,1)}, bf16[2,192,768]{2,1,0:T(8,128)(2,1)S(1)}, u32[]{:S(2)}, u32[]{:S(2)}) collective-permute-start(bf16[2,192,768]{2,1,0:T(8,128)(2,1)} %bitcast.456), channel_id=1, source_target_pairs={{0,4},{1,5},{2,6},{3,7},{4,0},{5,1},{6,2},{7,3},{8,12},{9,13},{10,... | collective-permute-start | bytes 1769480 | tf_op jit(solution)/shard_map/ppermute | solution.py:445
  231.0 32.5 %collective-permute-start.47 = (bf16[2,192,1152]{2,1,0:T(8,128)(2,1)S(1)}, bf16[2,192,1152]{2,1,0:T(8,128)(2,1)S(1)}, u32[]{:S(2)}, u32[]{:S(2)}) collective-permute-start(bf16[2,192,1152]{2,1,0:T(8,128)(2,1)S(1)} %pad_maximum_fusion.9), channel_id=1, source_target_pairs={{0,4},{1,5},{2,6},{3,7},{4,0},{5,1},{6,2},{7,3},{8,12},{9,13},{10,... | collective-permute-start | bytes 2654216 | tf_op jit(solution)/shard_map/ppermute | solution.py:445
  236.8 24.8 %collective-permute-start.42 = (bf16[1,192,1152]{2,1,0:T(8,128)(2,1)S(1)}, bf16[1,192,1152]{2,1,0:T(8,128)(2,1)S(1)}, u32[]{:S(2)}, u32[]{:S(2)}) collective-permute-start(bf16[1,192,1152]{2,1,0:T(8,128)(2,1)S(1)} %pad_maximum_fusion.23), channel_id=1, source_target_pairs={{0,4},{1,5},{2,6},{3,7},{4,0},{5,1},{6,2},{7,3},{8,12},{9,13},{10,... | collective-permute-start | bytes 1327112 | tf_op jit(solution)/shard_map/ppermute | solution.py:445
  238.4 24.1 %collective-permute-start.45 = (bf16[1,384,768]{2,1,0:T(8,128)(2,1)S(1)}, bf16[1,384,768]{2,1,0:T(8,128)(2,1)S(1)}, u32[]{:S(2)}, u32[]{:S(2)}) collective-permute-start(bf16[1,384,768]{2,1,0:T(8,128)(2,1)S(1)} %bitcast.457), channel_id=1, source_target_pairs={{0,1},{1,0},{2,3},{3,2},{4,5},{5,4},{6,7},{7,6},{8,9},{9,8},{10,11... | collective-permute-start | bytes 1769480 | tf_op jit(solution)/shard_map/ppermute | solution.py:445
  280.5 68.4 %collective-permute-start.57 = (f32[48,1536]{1,0:T(8,128)}, f32[48,1536]{1,0:T(8,128)}, u32[]{:S(2)}, u32[]{:S(2)}) collective-permute-start(f32[48,1536]{1,0:T(8,128)} %get-tuple-element.313), channel_id=1, source_target_pairs={{0,16},{1,17},{2,18},{3,19},{4,20},{5,21},{6,22},{7,23},{8,24},{9,... | collective-permute-start | bytes 884744 | tf_op jit(solution)/shard_map/ppermute | solution.py:445
  280.6 82.3 %collective-permute-start.60 = (f32[48,1536]{1,0:T(8,128)}, f32[48,1536]{1,0:T(8,128)}, u32[]{:S(2)}, u32[]{:S(2)}) collective-permute-start(f32[48,1536]{1,0:T(8,128)} %get-tuple-element.312), channel_id=1, source_target_pairs={{0,24},{1,25},{2,26},{3,27},{4,28},{5,29},{6,30},{7,31},{8,16},{9,... | collective-permute-start | bytes 884744 | tf_op jit(solution)/shard_map/ppermute | solution.py:445
  288.3 20.1 %collective-permute-start.50 = (bf16[1,192,1152]{2,1,0:T(8,128)(2,1)}, bf16[1,192,1152]{2,1,0:T(8,128)(2,1)S(1)}, u32[]{:S(2)}, u32[]{:S(2)}) collective-permute-start(bf16[1,192,1152]{2,1,0:T(8,128)(2,1)} %pad_maximum_fusion.24), channel_id=1, source_target_pairs={{0,1},{1,0},{2,3},{3,2},{4,5},{5,4},{6,7},{7,6},{8,9},{9,8},{10,11... | collective-permute-start | bytes 1327112 | tf_op jit(solution)/shard_map/ppermute | solution.py:445
  293.8 25.6 %collective-permute-start.52 = (bf16[1,384,1152]{2,1,0:T(8,128)(2,1)}, bf16[1,384,1152]{2,1,0:T(8,128)(2,1)S(1)}, u32[]{:S(2)}, u32[]{:S(2)}) collective-permute-start(bf16[1,384,1152]{2,1,0:T(8,128)(2,1)} %bitcast.440), channel_id=1, source_target_pairs={{0,1},{1,0},{2,3},{3,2},{4,5},{5,4},{6,7},{7,6},{8,9},{9,8},{10,11... | collective-permute-start | bytes 2654216 | tf_op jit(solution)/shard_map/ppermute | solution.py:445
  311.2 20.9 %collective-permute-start.51 = (bf16[4,48,1536]{2,1,0:T(8,128)(2,1)}, bf16[4,48,1536]{2,1,0:T(8,128)(2,1)}, u32[]{:S(2)}, u32[]{:S(2)}) collective-permute-start(bf16[4,48,1536]{2,1,0:T(8,128)(2,1)} %select_convert_fusion.1), channel_id=1, source_target_pairs={{0,8},{1,9},{2,10},{3,11},{4,12},{5,13},{6,14},{7,15},{8,0},{9,1},... | collective-permute-start | bytes 1769480 | tf_op jit(solution)/shard_map/ppermute | solution.py:445
  321.5 26.2 %collective-permute-start.58 = (bf16[1,192,1152]{2,1,0:T(8,128)(2,1)}, bf16[1,192,1152]{2,1,0:T(8,128)(2,1)}, u32[]{:S(2)}, u32[]{:S(2)}) collective-permute-start(bf16[1,192,1152]{2,1,0:T(8,128)(2,1)} %slice.730), channel_id=1, source_target_pairs={{0,4},{1,5},{2,6},{3,7},{4,0},{5,1},{6,2},{7,3},{8,12},{9,13},{10,... | collective-permute-start | bytes 1327112 | tf_op jit(solution)/shard_map/ppermute | solution.py:445
  334.8 26.6 %collective-permute-start.54 = (bf16[4,48,1536]{2,1,0:T(8,128)(2,1)}, bf16[4,48,1536]{2,1,0:T(8,128)(2,1)}, u32[]{:S(2)}, u32[]{:S(2)}) collective-permute-start(bf16[4,48,1536]{2,1,0:T(8,128)(2,1)} %fusion.176), channel_id=1, source_target_pairs={{8,24},{9,25},{10,26},{11,27},{12,28},{13,29},{14,30},{15,31},{16,... | collective-permute-start | bytes 1769480 | tf_op jit(solution)/shard_map/ppermute | solution.py:1226
  445.6 42.3 %collective-permute-start.75 = (bf16[48,1664]{1,0:T(8,128)(2,1)S(1)}, bf16[48,1664]{1,0:T(8,128)(2,1)S(1)}, u32[]{:S(2)}, u32[]{:S(2)}) collective-permute-start(bf16[48,1664]{1,0:T(8,128)(2,1)S(1)} %get-tuple-element.358), channel_id=1, source_target_pairs={{0,24},{1,25},{2,26},{3,27},{4,28},{5,29},{6,30},{7,31},{8,16},{9,... | collective-permute-start | bytes 479240 | tf_op jit(solution)/shard_map/ppermute | solution.py:445
  488.0 24.9 %collective-permute-start.76 = (bf16[48,3072]{1,0:T(8,128)(2,1)S(1)}, bf16[48,3072]{1,0:T(8,128)(2,1)S(1)}, u32[]{:S(2)}, u32[]{:S(2)}) collective-permute-start(bf16[48,3072]{1,0:T(8,128)(2,1)S(1)} %get-tuple-element.303), channel_id=1, source_target_pairs={{0,8},{1,9},{2,10},{3,11},{4,12},{5,13},{6,14},{7,15},{8,0},{9,1},... | collective-permute-start | bytes 884744 | tf_op jit(solution)/shard_map/ppermute | solution.py:445
  488.1 24.8 %collective-permute-start.77 = (bf16[48,3072]{1,0:T(8,128)(2,1)S(1)}, bf16[48,3072]{1,0:T(8,128)(2,1)S(1)}, u32[]{:S(2)}, u32[]{:S(2)}) collective-permute-start(bf16[48,3072]{1,0:T(8,128)(2,1)S(1)} %get-tuple-element.302), channel_id=1, source_target_pairs={{0,16},{1,17},{2,18},{3,19},{4,20},{5,21},{6,22},{7,23},{8,24},{9,... | collective-permute-start | bytes 884744 | tf_op jit(solution)/shard_map/ppermute | solution.py:445
  491.0 26.2 %collective-permute-start.78 = (bf16[48,3072]{1,0:T(8,128)(2,1)S(1)}, bf16[48,3072]{1,0:T(8,128)(2,1)S(1)}, u32[]{:S(2)}, u32[]{:S(2)}) collective-permute-start(bf16[48,3072]{1,0:T(8,128)(2,1)S(1)} %get-tuple-element.301), channel_id=1, source_target_pairs={{0,24},{1,25},{2,26},{3,27},{4,28},{5,29},{6,30},{7,31},{8,16},{9,... | collective-permute-start | bytes 884744 | tf_op jit(solution)/shard_map/ppermute | solution.py:445
  (201 other events, 1391.1 us)
